TPU v7x, 256 devices: a whole 4x4x8 slice. The times are simulated.
256 devices in a mesh: row: 8 (over z), col: 32 (over x, y, core).
Axes of the slice: x: 4, y: 4, z: 8, core: 2. Of those that a mesh axis runs over, the one named last changes fastest.
Arguments:
- kernel: float32 [12, 1024, 3, 4096], P(None, 'row', None, 'col'), may hold values from -0.25 to 3, as said below
Outputs:
- factored: float32 [12, 1024, 3, 4096], P(None, 'row', None, 'col')
Inputs may be any that keep to these rules, and one draw needn't show every extreme that they name: kernel is symmetric positive definite; diagonal entries lie in 2 to 3 and off-diagonal entries in -0.25 to 1.25.
All inputs are finite; a program needn't handle non-finite values.
Results may differ from a plain program's by a relative error of at most 0.0003.
Values sent between devices are 32-bit elements; how exact they have to be, the bound alone decides.
No kernel may reach another device: no remote copies, remote signals or barrier semaphores. Data moves between devices by JAX's collectives and lax.ppermute only.
A program may use at most 64 MiB of HBM per device.

v0:
```python
import jax
import jax.numpy as jnp
from jax import lax
from jax.sharding import PartitionSpec as P


def broadcast(value, axis, source):
    kept = jnp.where(lax.axis_index(axis) == source, value, 0).astype(value.dtype)
    return lax.psum(kept, axis)


def shards(kernel):
    tile_rows, tile, tile_cols, _ = kernel.shape
    nrows = lax.axis_size("row")
    ncols = lax.axis_size("col")
    my_row = lax.axis_index("row")
    my_col = lax.axis_index("col")
    rows_glob = jnp.arange(tile_rows, dtype=jnp.int32) * nrows + my_row
    cols_glob = jnp.arange(tile_cols, dtype=jnp.int32) * ncols + my_col
    work = kernel
    for k in range(2):
        local_s = k // nrows
        local_t = k // ncols
        diag = broadcast(work[local_s, :, local_t, :], "row", k % nrows)
        lower = jnp.linalg.cholesky(diag)
        column = work[:, :, local_t, :].reshape(tile_rows * tile, tile)
        solved = lax.linalg.triangular_solve(
            lower, column, left_side=False, lower=True, transpose_a=True
        )
        solved = solved.reshape(tile_rows, tile, tile)
        below = (rows_glob > k)[:, None, None]
        onrow = (rows_glob == k)[:, None, None]
        panel = jnp.where(below, solved, jnp.where(onrow, jnp.tril(lower)[None], jnp.float32(0.0)))
        gathered = lax.all_gather(panel[:, None], "row", axis=1, tiled=True)
        spread = broadcast(gathered, "col", k % ncols)
        mine_rows = lax.dynamic_index_in_dim(spread, my_row, 1, keepdims=False)
        flat = spread.reshape(tile_cols, ncols, tile, tile)
        mine_cols = lax.dynamic_index_in_dim(flat, my_col, 1, keepdims=False)
        left_part = jnp.where((rows_glob > k)[:, None, None], mine_rows, jnp.float32(0.0))
        right_part = jnp.where((cols_glob > k)[:, None, None], mine_cols, jnp.float32(0.0))
        update = jnp.einsum("sai,tbi->satb", left_part, right_part, precision=lax.Precision.HIGHEST)
        work = work - update
        column_mask = (cols_glob == k)[None, None, :, None]
        work = jnp.where(column_mask, mine_rows[:, :, None, :], work)
        row_mask = (rows_glob == k)[:, None, None, None] & (cols_glob > k)[None, None, :, None]
        work = jnp.where(row_mask, jnp.float32(0.0), work)
    return work


def solution(mesh):
    return jax.shard_map(
        shards,
        mesh=mesh,
        in_specs=(P(None, "row", None, "col"),),
        out_specs=P(None, "row", None, "col"),
        check_vma=False,
    )
```

profile of v0, /device:TPU:200, one launch (start us, length us, event | category | flops | bytes accessed | tf_op | source)
XLA Modules:
  0.0 644.0 jit_solution(14572059811042640961)
XLA Ops:
  6.5 2.1 copy.25
  9.5 70.3 %all-reduce.5.cloned.1.call-done = f32[128,128]{0,1:T(8,128)} async-done(((f32[128,128]{0,1:T(8,128)}), f32[128,128]{0,1:T(8,128)}) %all-reduce.5.cloned.1.call-update) | async-done | bytes 65552 | tf_op jit(solution)/shard_map/psum | solution.py:9
  79.8 0.9 copy.26
  80.7 0.9 fusion.25
  81.5 11.7 %cholesky.44 = f32[128,128]{1,0:T(8,128)S(1)} custom-call(f32[128,128]{1,0:T(8,128)S(1)} %fusion.25), custom_call_target="Cholesky" | custom-call | tf_op jit(solution)/shard_map/jit(cholesky)/cholesky | solution.py:25
  95.3 9.8 %custom-call.6 = f32[1,128,128]{1,2,0:T(8,128)S(1)} custom-call(f32[1,128,128]{2,1,0:T(8,128)S(1)} %fusion.35), custom_call_target="InvertDiagBlocksLowerTriangular" | custom-call | tf_op jit(solution)/shard_map/triangular_solve/custom-call.0 | solution.py:27
  105.1 1.8 convolution_bitcast_fusion.1
  106.9 1.4 copy.27
  108.3 1.1 select_select_fusion.3
  109.4 73.2 %all-gather.3.cloned.1.call-done = f32[12,8,128,128]{3,2,0,1:T(8,128)} async-done(((f32[12,1,128,128]{3,2,0,1:T(8,128)}), f32[12,8,128,128]{3,2,0,1:T(8,128)}) %all-gather.3.cloned.1.call-update) | async-done | bytes 6291472 | tf_op jit(solution)/shard_map/all_gather | solution.py:34
  182.6 3.7 broadcast_select_fusion.1
  186.5 125.6 %all-reduce.7.cloned.1.call-done = f32[12,8,128,128]{3,2,0,1:T(8,128)} async-done(((f32[12,8,128,128]{3,2,0,1:T(8,128)}), f32[12,8,128,128]{3,2,0,1:T(8,128)}) %all-reduce.7.cloned.1.call-update) | async-done | bytes 6291472 | tf_op jit(solution)/shard_map/psum | solution.py:9
  312.1 1.2 dynamic-slice_bitcast_fusion.1
  313.6 3.4 copy.29
  317.0 3.5 select_select_fusion.1
  321.4 0.9 slice.24
  322.4 1.4 copy.33
  323.8 67.5 %all-reduce.9.cloned.1.call-done = f32[128,128]{0,1:T(8,128)} async-done(((f32[128,128]{0,1:T(8,128)}), f32[128,128]{0,1:T(8,128)}) %all-reduce.9.cloned.1.call-update) | async-done | bytes 65552 | tf_op jit(solution)/shard_map/psum | solution.py:9
  391.3 0.9 copy.32
  393.1 11.7 %cholesky.55 = f32[128,128]{1,0:T(8,128)S(1)} custom-call(f32[128,128]{1,0:T(8,128)S(1)} %fusion.23), custom_call_target="Cholesky" | custom-call | tf_op jit(solution)/shard_map/jit(cholesky)/cholesky | solution.py:25
  406.8 9.8 %custom-call.7 = f32[1,128,128]{1,2,0:T(8,128)S(1)} custom-call(f32[1,128,128]{2,1,0:T(8,128)S(1)} %fusion.34), custom_call_target="InvertDiagBlocksLowerTriangular" | custom-call | tf_op jit(solution)/shard_map/triangular_solve/custom-call.0 | solution.py:27
  416.6 1.7 convolution_bitcast_fusion
  418.3 1.4 copy.34
  419.7 1.1 select_select_fusion.2
  420.9 73.2 %all-gather.5.cloned.1.call-done = f32[12,8,128,128]{3,2,0,1:T(8,128)} async-done(((f32[12,1,128,128]{3,2,0,1:T(8,128)}), f32[12,8,128,128]{3,2,0,1:T(8,128)}) %all-gather.5.cloned.1.call-update) | async-done | bytes 6291472 | tf_op jit(solution)/shard_map/all_gather | solution.py:34
  494.1 3.7 broadcast_select_fusion
  497.9 125.6 %all-reduce.11.cloned.1.call-done = f32[12,8,128,128]{3,2,0,1:T(8,128)} async-done(((f32[12,8,128,128]{3,2,0,1:T(8,128)}), f32[12,8,128,128]{3,2,0,1:T(8,128)}) %all-reduce.11.cloned.1.call-update) | async-done | bytes 6291472 | tf_op jit(solution)/shard_map/psum | solution.py:9
  623.5 1.2 dynamic-slice_bitcast_fusion
  624.7 1.1 copy.35
  625.9 3.3 copy.36
  629.2 4.9 select_select_fusion
  634.1 3.0 copy.38
  (39 shorter events, 7.3 us)
Async XLA Ops:
  6.5 98.6 %slice-start = ((f32[12,128,3,128]{3,1,2,0:T(8,128)}), f32[12,128,1,128]{3,1,2,0:T(8,128)S(1)}, s32[]{:S(2)}) async-start(f32[12,128,3,128]{3,1,2,0:T(8,128)} %param.4), calls=%async_computation.6 | async-start | bytes 1572864 | tf_op jit(solution)/shard_map/slice | solution.py:26
  6.5 73.2 %all-reduce.5.cloned.1.call-start = ((), (), s32[]{:S(2)}) async-start(), calls=%async_computation | async-start | bytes 131072 | tf_op jit(solution)/shard_map/psum | solution.py:9
  8.7 177.7 %copy-start = (f32[12,128,3,128]{1,3,2,0:T(8,128)}, f32[12,128,3,128]{1,3,2,0:T(8,128)S(1)}, u32[]{:S(2)}) copy-start(f32[12,128,3,128]{1,3,2,0:T(8,128)S(1)} %copy.25) | copy-start | bytes 7077892
  9.4 173.2 %all-gather.3.cloned.1.call-start = ((), (), s32[]{:S(2)}) async-start(), calls=%async_computation.1 | async-start | bytes 7077888 | tf_op jit(solution)/shard_map/all_gather | solution.py:34
  109.4 202.7 %all-reduce.7.cloned.1.call-start = ((), (), s32[]{:S(2)}) async-start(), calls=%async_computation.2 | async-start | bytes 12582912 | tf_op jit(solution)/shard_map/psum | solution.py:9
  186.4 204.9 %all-reduce.9.cloned.1.call-start = ((), (), s32[]{:S(2)}) async-start(), calls=%async_computation.3 | async-start | bytes 131072 | tf_op jit(solution)/shard_map/psum | solution.py:9
  313.6 3.5 copy-start.1
  321.2 172.9 %all-gather.5.cloned.1.call-start = ((), (), s32[]{:S(2)}) async-start(), calls=%async_computation.4 | async-start | bytes 7077888 | tf_op jit(solution)/shard_map/all_gather | solution.py:34
  420.8 202.7 %all-reduce.11.cloned.1.call-start = ((), (), s32[]{:S(2)}) async-start(), calls=%async_computation.5 | async-start | bytes 12582912 | tf_op jit(solution)/shard_map/psum | solution.py:9
  625.9 3.3 copy-start.2
Sparse Core Ops, SparseCore 0:
  9.7 70.0 all-reduce.4
  109.5 73.0 all-gather.2
  186.5 125.5 all-reduce.6
  321.3 69.9 all-reduce.8
  421.0 73.0 all-gather.4
  497.9 125.5 all-reduce.10
where the time goes:
time: 649 us; the launch traced here: 644 us
  waiting for transfers between devices  535 us (82%)
  other arithmetic  59.9 us (9%)
  local copies, waits for them, and re-layouts  22.7 us (3%)
  between operations  13.7 us (2%)
  matrix products  11.9 us (2%)
    psum x4, waiting for transfers between devices, broadcast(): return lax.psum(kept, axis)  389 us
    all_gather x2, waiting for transfers between devices, shards(): gathered = lax.all_gather(panel[:, None], 'row', axis=1, tiled=True)  146 us
    another operation x6, other arithmetic, shards(): lower = jnp.linalg.cholesky(diag)  24.8 us
    another operation x6, other arithmetic, shards(): lax.linalg.triangular_solve(lower, column, left_side=False, lower=True, t...  22.2 us
  transfers between devices with their start and end apart: 6, of which 6 were waited for; matrix products, arithmetic and copies ran while one was open for 0% of the time, Pallas kernels for 0%

commit v1 on v0

v1 whole, which is shorter than its diff:
```python
import functools

import jax
import jax.numpy as jnp
from jax import lax
from jax.experimental import pallas as pl
from jax.experimental.pallas import tpu as pltpu
from jax.sharding import PartitionSpec as P

TB = 128
ROWS = 8
SIDE = 4
ROW_TILES = 12
COL_TILES = 3
HIGHEST = lax.Precision.HIGHEST


def col_of(x, y, core):
    return (x * SIDE + y) * 2 + core


def device_of(z, col):
    return z * SIDE * SIDE * 2 + col


def send(value, pairs):
    return lax.ppermute(value, ("row", "col"), pairs)


def inverse_factor(tile, beside):
    lane = lax.broadcasted_iota(jnp.int32, (8, TB), 1)
    sub = lax.broadcasted_iota(jnp.int32, (8, TB), 0)
    groups = TB // 8
    rows = [tile[8 * g : 8 * g + 8, :] for g in range(groups)]

    def across(value, k):
        return jnp.broadcast_to(value[:, k : k + 1], (8, TB))

    def down(value, k):
        return jnp.broadcast_to(value[k : k + 1, :], (8, TB))

    for p in range(groups):
        first = 8 * p
        wide = {g: [across(rows[g], first + k) for k in range(8)] for g in range(p, groups)}
        inside = (lane >= first) & (lane < first + 8)
        rows[p] = jnp.where(inside, jnp.where(lane - first == sub, 1.0, 0.0), rows[p])
        for g in range(p + 1, groups):
            rows[g] = jnp.where(inside, 0.0, rows[g])
        mine = wide[p]
        coef = {}
        scale = []
        top = []
        for k in range(8):
            r = lax.rsqrt(down(mine[k], k))
            scale.append(r)
            column = jnp.where(sub > k, mine[k] * r, 0.0)
            for m in range(k + 1, 8):
                coef[k, m] = down(mine[m], k) * r
                mine[m] = mine[m] - column * coef[k, m]
            u = down(rows[p], k) * r
            top.append(u)
            rows[p] = jnp.where(sub == k, u, rows[p] - column * u)
        for g in range(p + 1, groups):
            columns = []
            for k in range(8):
                value = wide[g][k]
                for m in range(k):
                    value = value - columns[m] * coef[m, k]
                columns.append(value * scale[k])
            total = rows[g]
            for k in range(8):
                total = total - columns[k] * top[k]
            rows[g] = total
        beside(p)
    return jnp.concatenate([jnp.where(lane <= sub + 8 * g, rows[g], 0.0) for g in range(groups)], axis=0)


def halves(value):
    high = value.astype(jnp.bfloat16)
    return high, (value - high.astype(jnp.float32)).astype(jnp.bfloat16)


def product(a, b, transposed):
    dims = (((1,), (1 if transposed else 0,)), ((), ()))
    dot = functools.partial(lax.dot_general, dimension_numbers=dims, preferred_element_type=jnp.float32)
    return dot(a[0], b[0]) + (dot(a[0], b[1]) + dot(a[1], b[0]))


def exact(a, b, transposed=False):
    dims = (((1,), (1 if transposed else 0,)), ((), ()))
    return lax.dot_general(a, b, dims, precision=HIGHEST, preferred_element_type=jnp.float32)


def factor_and_update(
    place, d00, d01, d11, even, odd, near, far, kernel, out, r_high, r_low, block, in_sem, out_sem
):
    my_row, my_col = place[0], place[1]
    my_x = my_col // (2 * SIDE)
    swapped = lax.rem(my_col, 2) != lax.rem(my_row, 2)
    load = pltpu.make_async_copy(kernel, block, in_sem)
    load.start()

    def turn(s):
        piece = lax.rem(my_x - s % SIDE + SIDE, SIDE)
        a = near[piece, s // SIDE]
        b = far[piece, s // SIDE]
        first = jnp.where(swapped, b, a).T
        second = jnp.where(swapped, a, b).T
        for k, value in enumerate((first, second)):
            high, low = halves(value)
            r_high[s * TB : (s + 1) * TB, k * TB : (k + 1) * TB] = high
            r_low[s * TB : (s + 1) * TB, k * TB : (k + 1) * TB] = low

    def nothing(p):
        pass

    def beside(p):
        if p < ROW_TILES:
            turn(p)

    is_odd = lax.rem(my_row, 2) == 1
    a01 = d01[...]
    a10 = jnp.where(is_odd, a01, a01.T)
    inv00 = inverse_factor(d00[...], beside)
    l10 = exact(a10, inv00, transposed=True)
    schur = d11[...] - exact(l10, l10, transposed=True)
    mixed = exact(l10, inv00)
    inv11 = inverse_factor(schur, nothing)
    inv10 = -exact(inv11, mixed)
    inverse = jnp.concatenate(
        [
            jnp.concatenate([inv00, jnp.zeros((TB, TB), jnp.float32)], axis=1),
            jnp.concatenate([inv10, inv11], axis=1),
        ],
        axis=0,
    )
    inv = halves(inverse)
    top = jnp.concatenate(
        [
            jnp.concatenate([even[t] for t in range(COL_TILES)], axis=1),
            jnp.concatenate([odd[t] for t in range(COL_TILES)], axis=1),
        ],
        axis=0,
    )
    right = halves(product(inv, halves(top), False))

    lane = lax.broadcasted_iota(jnp.int32, (TB, TB), 1)
    sub = lax.broadcasted_iota(jnp.int32, (TB, TB), 0)
    load.wait()
    for s in range(ROW_TILES):
        rows = slice(s * TB, (s + 1) * TB)
        left = product((r_high[rows, :], r_low[rows, :]), inv, True)
        update = product(halves(left), right, False)
        for t in range(COL_TILES):
            block[s, t] = block[s, t] - update[:, t * TB : (t + 1) * TB]

        @pl.when(my_col == 0)
        def _():
            block[s, 0] = left[:, :TB]

        @pl.when(my_col == 1)
        def _():
            block[s, 0] = left[:, TB:]

        if s == 0:
            keep = lane <= sub

            @pl.when(my_row < 2)
            def _():
                for t in range(1, COL_TILES):
                    block[0, t] = jnp.zeros((TB, TB), jnp.float32)

                @pl.when((my_col > 1) | (my_row < my_col))
                def _():
                    block[0, 0] = jnp.zeros((TB, TB), jnp.float32)

                @pl.when(my_row == my_col)
                def _():
                    block[0, 0] = jnp.where(keep, block[0, 0], 0.0)

        pltpu.make_async_copy(block.at[s], out.at[s], out_sem.at[s]).start()
    for s in range(ROW_TILES):
        pltpu.make_async_copy(block.at[s], out.at[s], out_sem.at[s]).wait()


def shards(kernel):
    my_row = lax.axis_index("row").astype(jnp.int32)
    my_col = lax.axis_index("col").astype(jnp.int32)
    my_x = my_col // (2 * SIDE)
    my_y = (my_col // 2) % SIDE
    my_core = my_col % 2
    odd_row = my_row % 2 == 1
    tiles = kernel.transpose(0, 2, 1, 3)
    head = tiles[0]

    cols = range(2 * SIDE * SIDE)
    zs = range(ROWS)
    sides = range(SIDE)
    cores = range(2)

    diag = head[0]
    with jax.named_scope("diag_z"):
        got = send(diag, [(device_of(z, c), device_of(z + 4, c)) for z in (0, 1) for c in cores])
        diag = jnp.where((my_row == 4) | (my_row == 5), got, diag)
        got = send(diag, [(device_of(z, c), device_of(z + 2, c)) for z in (0, 1, 4, 5) for c in cores])
        diag = jnp.where(my_row % 4 >= 2, got, diag)
    with jax.named_scope("diag_x"):
        got = send(diag, [(device_of(z, col_of(0, 0, c)), device_of(z, col_of(2, 0, c))) for z in zs for c in cores])
        diag = jnp.where(my_x == 2, got, diag)
        got = send(
            diag,
            [(device_of(z, col_of(x, 0, c)), device_of(z, col_of(x + 1, 0, c))) for z in zs for x in (0, 2) for c in cores],
        )
        diag = jnp.where(my_x % 2 == 1, got, diag)
    with jax.named_scope("diag_y"):
        got = send(
            diag,
            [(device_of(z, col_of(x, 0, c)), device_of(z, col_of(x, 2, c))) for z in zs for x in sides for c in cores],
        )
        diag = jnp.where(my_y == 2, got, diag)
        got = send(
            diag,
            [
                (device_of(z, col_of(x, y, c)), device_of(z, col_of(x, y + 1, c)))
                for z in zs
                for x in sides
                for y in (0, 2)
                for c in cores
            ],
        )
        diag = jnp.where(my_y % 2 == 1, got, diag)
    swap_core = [(device_of(z, c), device_of(z, c ^ 1)) for z in zs for c in cols]
    swap_row = [(device_of(z, c), device_of(z ^ 1, c)) for z in zs for c in cols]
    with jax.named_scope("diag_swap"):
        other = send(diag, swap_core)
        left = jnp.where(my_core == 0, diag, other)
        right = jnp.where(my_core == 0, other, diag)
        mine = jnp.where(odd_row, right, left)
        theirs = send(mine, swap_row)
        d00 = jnp.where(odd_row, theirs, mine)
        d11 = jnp.where(odd_row, mine, theirs)
        d01 = jnp.where(odd_row, left, right)

    with jax.named_scope("cols"):
        part = head
        got = send(part, [(device_of(z, c), device_of(z + 4, c)) for z in (0, 1) for c in cols])
        part = jnp.where((my_row == 4) | (my_row == 5), got, part)
        got = send(part, [(device_of(z, c), device_of(z + 2, c)) for z in (0, 1, 4, 5) for c in cols])
        part = jnp.where(my_row % 4 >= 2, got, part)
        other_part = send(part, swap_row)
        even = jnp.where(odd_row, other_part, part)
        odd = jnp.where(odd_row, part, other_part)

    with jax.named_scope("rows"):
        home = my_row // 2
        piece = send(
            head,
            [(device_of(0, c), device_of(c % ROWS, c)) for c in cols]
            + [(device_of(1, c), device_of(c % ROWS, c ^ 1)) for c in cols],
        )

        def along_y(starts, step):
            return [
                (
                    device_of(z, col_of(x, (z // 2 + start) % SIDE, c)),
                    device_of(z, col_of(x, (z // 2 + start + step) % SIDE, c)),
                )
                for z in zs
                for x in sides
                for start in starts
                for c in cores
            ]

        def along_x(step):
            return [
                (device_of(z, col_of(x, y, c)), device_of(z, col_of((x + step) % SIDE, y, c)))
                for z in zs
                for x in sides
                for y in sides
                for c in cores
            ]

        got = send(piece, along_y((0,), 2))
        piece = jnp.where((my_y - home) % SIDE == 2, got, piece)
        got = send(piece, along_y((0, 2), 1))
        piece = jnp.where((my_y - home) % SIDE % 2 == 1, got, piece)
        up = send(piece, along_x(1))
        down = send(piece, along_x(-1))
        up2 = send(up, along_x(1))
        near = jnp.stack([piece, up, up2, down])
        far = send(near, swap_core)

    place = jnp.stack([my_row, my_col])
    vmem = pl.BlockSpec(memory_space=pltpu.VMEM)
    anywhere = pl.BlockSpec(memory_space=pl.ANY)
    result = pl.pallas_call(
        factor_and_update,
        out_shape=jax.ShapeDtypeStruct(tiles.shape, tiles.dtype),
        in_specs=[pl.BlockSpec(memory_space=pltpu.SMEM)] + [vmem] * 7 + [anywhere],
        out_specs=anywhere,
        scratch_shapes=[
            pltpu.VMEM((ROW_TILES * TB, 2 * TB), jnp.bfloat16),
            pltpu.VMEM((ROW_TILES * TB, 2 * TB), jnp.bfloat16),
            pltpu.VMEM((ROW_TILES, COL_TILES, TB, TB), jnp.float32),
            pltpu.SemaphoreType.DMA,
            pltpu.SemaphoreType.DMA((ROW_TILES,)),
        ],
        compiler_params=pltpu.CompilerParams(vmem_limit_bytes=40 * 1024 * 1024),
        name="factor_and_update",
    )(place, d00, d01, d11, even, odd, near, far, tiles)
    return result.transpose(0, 2, 1, 3)


def solution(mesh):
    return jax.shard_map(
        shards,
        mesh=mesh,
        in_specs=(P(None, "row", None, "col"),),
        out_specs=P(None, "row", None, "col"),
        check_vma=False,
    )
```

time: 649 us -> 84.3 us (0.13)
  the two profiles are of different devices: /device:TPU:200 before, /device:TPU:24 now
where the time goes in v1:
time: 84.3 us; the launch traced here: 84 us
  waiting for transfers between devices  38 us (45%)
  starting transfers between devices  23.6 us (28%)
  Pallas kernels  18.7 us (22%)
  local copies, waits for them, and re-layouts  1.94 us (2%)
  other arithmetic  1.19 us (1%)
    ppermute x18, waiting for transfers between devices, send(): return lax.ppermute(value, ('row', 'col'), pairs)  38 us
    ppermute x18, starting transfers between devices, send(): return lax.ppermute(value, ('row', 'col'), pairs)  23.6 us
    pallas_call x1, Pallas kernels, shards(): pl.pallas_call(factor_and_update, out_shape=jax.ShapeDtypeStruct(tiles.sh...  18.7 us
  transfers between devices with their start and end apart: 18, of which 6 were waited for; matrix products, arithmetic and copies ran while one was open for 2% of the time, Pallas kernels for 0%

profile of v1, /device:TPU:24, one launch (start us, length us, event | category | flops | bytes accessed | tf_op | source)
XLA Modules:
  0.0 84.0 jit_solution(9237031840901213129)
XLA Ops:
  0.0 1.0 %slice_bitcast_fusion.1 = f32[128,128]{1,0:T(8,128)S(1)} fusion(f32[12,3,128,128]{3,2,1,0:T(8,128)} %bitcast.16), kind=kLoop, calls=%fused_computation.8 | loop fusion | bytes 131072 | tf_op jit(solution)/shard_map/squeeze | solution.py:201
  1.0 0.7 collective-permute-start
  1.7 0.0 collective-permute-done
  1.7 0.9 %broadcast_select_fusion.6 = f32[128,128]{1,0:T(8,128)S(1)} fusion(f32[128,128]{1,0:T(8,128)S(1)} %collective-permute-done, pred[]{:T(512)S(6)} %or.4, f32[12,3,128,128]{3,2,1,0:T(8,128)} %bitcast.17), kind=kLoop, calls=%fused_computation.9 | loop fusion | flops 16384 | bytes 196609 | tf_op jit(solution)/shard_map/diag_z/jit(_where)/select_n | solution.py:204
  2.5 0.7 collective-permute-start.1
  3.2 0.0 collective-permute-done.1
  3.2 0.7 collective-permute-start.2
  3.9 0.9 %slice_bitcast_fusion = f32[3,128,128]{2,1,0:T(8,128)S(1)} fusion(f32[12,3,128,128]{3,2,1,0:T(8,128)} %bitcast.18), kind=kLoop, calls=%fused_computation.1 | loop fusion | bytes 393216 | tf_op jit(solution)/shard_map/squeeze | solution.py:194
  4.9 8.2 %collective-permute-start.11 = (f32[3,128,128]{2,1,0:T(8,128)S(1)}, f32[3,128,128]{2,1,0:T(8,128)S(1)}, u32[]{:S(2)}, u32[]{:S(2)}) collective-permute-start(f32[3,128,128]{2,1,0:T(8,128)S(1)} %slice_bitcast_fusion), channel_id=1, source_target_pairs={{0,0},{1,33},{2,66},{3,99},{4,132},{5,165},{6,198},{7,231},{8,8},{... | collective-permute-start | bytes 589832 | tf_op jit(solution)/shard_map/rows/ppermute | solution.py:27
  13.1 1.6 %collective-permute-start.8 = (f32[3,128,128]{2,1,0:T(8,128)S(1)}, f32[3,128,128]{2,1,0:T(8,128)S(1)}, u32[]{:S(2)}, u32[]{:S(2)}) collective-permute-start(f32[3,128,128]{2,1,0:T(8,128)S(1)} %slice_bitcast_fusion), channel_id=1, source_target_pairs={{0,128},{1,129},{2,130},{3,131},{4,132},{5,133},{6,134},{7,135},{8... | collective-permute-start | bytes 589832 | tf_op jit(solution)/shard_map/cols/ppermute | solution.py:27
  14.8 0.7 collective-permute-start.3
  15.5 0.1 pad_add_fusion.place
  15.6 9.6 %collective-permute-done.11 = f32[3,128,128]{2,1,0:T(8,128)S(1)} collective-permute-done((f32[3,128,128]{2,1,0:T(8,128)S(1)}, f32[3,128,128]{2,1,0:T(8,128)S(1)}, u32[]{:S(2)}, u32[]{:S(2)}) %collective-permute-start.11) | collective-permute-done | bytes 196640 | tf_op jit(solution)/shard_map/rows/ppermute | solution.py:27
  25.2 0.7 collective-permute-start.12
  25.9 0.0 collective-permute-done.3
  25.9 0.7 collective-permute-start.4
  26.6 1.3 %collective-permute-start.13 = (f32[3,128,128]{2,1,0:T(8,128)S(1)}, f32[3,128,128]{2,1,0:T(8,128)S(1)}, u32[]{:S(2)}, u32[]{:S(2)}) collective-permute-start(f32[3,128,128]{2,1,0:T(8,128)S(1)} %broadcast_select_fusion), channel_id=1, source_target_pairs={{0,2},{1,3},{4,6},{5,7},{8,10},{9,11},{12,14},{13,15},{16,18},{17,... | collective-permute-start | bytes 589832 | tf_op jit(solution)/shard_map/rows/ppermute | solution.py:27
  27.9 1.3 %collective-permute-start.5 = (f32[128,128]{1,0:T(8,128)S(1)}, f32[128,128]{1,0:T(8,128)S(1)}, u32[]{:S(2)}, u32[]{:S(2)}) collective-permute-start(f32[128,128]{1,0:T(8,128)S(1)} %broadcast_select_fusion.10), channel_id=1, source_target_pairs={{0,2},{1,3},{4,6},{5,7},{8,10},{9,11},{12,14},{13,15},{16,18},{17,... | collective-permute-start | bytes 196616 | tf_op jit(solution)/shard_map/diag_y/ppermute | solution.py:27
  29.2 11.4 %collective-permute-done.13 = f32[3,128,128]{2,1,0:T(8,128)S(1)} collective-permute-done((f32[3,128,128]{2,1,0:T(8,128)S(1)}, f32[3,128,128]{2,1,0:T(8,128)S(1)}, u32[]{:S(2)}, u32[]{:S(2)}) %collective-permute-start.13) | collective-permute-done | bytes 196640 | tf_op jit(solution)/shard_map/rows/ppermute | solution.py:27
  40.7 0.1 collective-permute-start.14
  40.8 1.3 %collective-permute-start.9 = (f32[3,128,128]{2,1,0:T(8,128)S(1)}, f32[3,128,128]{2,1,0:T(8,128)S(1)}, u32[]{:S(2)}, u32[]{:S(2)}) collective-permute-start(f32[3,128,128]{2,1,0:T(8,128)S(1)} %broadcast_select_fusion.2), channel_id=1, source_target_pairs={{0,64},{1,65},{2,66},{3,67},{4,68},{5,69},{6,70},{7,71},{8,72},{9,... | collective-permute-start | bytes 589832 | tf_op jit(solution)/shard_map/cols/ppermute | solution.py:27
  42.1 3.3 %collective-permute-start.16 = (f32[3,128,128]{2,1,0:T(8,128)S(1)}, f32[3,128,128]{2,1,0:T(8,128)S(1)}, u32[]{:S(2)}, u32[]{:S(2)}) collective-permute-start(f32[3,128,128]{2,1,0:T(8,128)S(1)} %broadcast_select_fusion.1), channel_id=1, source_target_pairs={{0,24},{1,25},{2,26},{3,27},{4,28},{5,29},{6,30},{7,31},{8,0},{9,1... | collective-permute-start | bytes 589832 | tf_op jit(solution)/shard_map/rows/ppermute | solution.py:27
  45.4 3.7 %collective-permute-done.14 = f32[3,128,128]{2,1,0:T(8,128)S(1)} collective-permute-done((f32[3,128,128]{2,1,0:T(8,128)S(1)}, f32[3,128,128]{2,1,0:T(8,128)S(1)}, u32[]{:S(2)}, u32[]{:S(2)}) %collective-permute-start.14) | collective-permute-done | bytes 196640 | tf_op jit(solution)/shard_map/rows/ppermute | solution.py:27
  49.1 0.1 collective-permute-start.6
  49.2 6.7 %collective-permute-done.15 = f32[3,128,128]{2,1,0:T(8,128)S(1)} collective-permute-done((f32[3,128,128]{2,1,0:T(8,128)S(1)}, f32[3,128,128]{2,1,0:T(8,128)S(1)}, u32[]{:S(2)}, u32[]{:S(2)}) %collective-permute-start.15) | collective-permute-done | bytes 196640 | tf_op jit(solution)/shard_map/rows/ppermute | solution.py:27
  56.0 0.1 pad_maximum_fusion.near
  56.0 0.1 collective-permute-start.17
  56.1 1.6 %collective-permute-start.7 = (f32[128,128]{1,0:T(8,128)S(1)}, f32[128,128]{1,0:T(8,128)S(1)}, u32[]{:S(2)}, u32[]{:S(2)}) collective-permute-start(f32[128,128]{1,0:T(8,128)S(1)} %get-tuple-element.10), channel_id=1, source_target_pairs={{0,32},{1,33},{2,34},{3,35},{4,36},{5,37},{6,38},{7,39},{8,40},{9,... | collective-permute-start | bytes 196616 | tf_op jit(solution)/shard_map/diag_swap/ppermute | solution.py:27
  57.8 0.8 collective-permute-start.10
  58.6 2.2 %collective-permute-done.7 = f32[128,128]{1,0:T(8,128)S(1)} collective-permute-done((f32[128,128]{1,0:T(8,128)S(1)}, f32[128,128]{1,0:T(8,128)S(1)}, u32[]{:S(2)}, u32[]{:S(2)}) %collective-permute-start.7) | collective-permute-done | bytes 65568 | tf_op jit(solution)/shard_map/diag_swap/ppermute | solution.py:27
  60.7 4.3 %collective-permute-done.10 = f32[3,128,128]{2,1,0:T(8,128)S(1)} collective-permute-done((f32[3,128,128]{2,1,0:T(8,128)S(1)}, f32[3,128,128]{2,1,0:T(8,128)S(1)}, u32[]{:S(2)}, u32[]{:S(2)}) %collective-permute-start.10) | collective-permute-done | bytes 196640 | tf_op jit(solution)/shard_map/cols/ppermute | solution.py:27
  65.1 18.7 %factor_and_update.1 = f32[12,3,128,128]{3,2,1,0:T(8,128)} custom-call(s32[2]{0:T(128)S(1)} %pad_add_fusion.place, f32[128,128]{1,0:T(8,128)S(1)} %get-tuple-element.8.d00, f32[128,128]{1,0:T(8,128)S(1)} %get-tuple-element.9.d01, f32[128,128]{1,0:T(8,128)S(1)} %get-tuple-element.7.d11, f32[3,128,128]{2,1,0:T(8,128)S(1)} %get-tuple-element.6.even, ...), custom_call_target="tpu_custom_call" | custom-call | tf_op jit(solution)/shard_map/factor_and_update/pallas_call | solution.py:296
  (24 shorter events, 0.2 us)
Async XLA Ops:
  0.0 40.8 %copy-start = (f32[12,128,3,128]{3,1,2,0:T(8,128)S(1)}, f32[12,128,3,128]{3,1,2,0:T(8,128)}, u32[]{:S(2)}) copy-start(f32[12,128,3,128]{3,1,2,0:T(8,128)} %param.1) | copy-start | bytes 7077892
  1.0 0.7 collective-permute-start
  2.5 0.7 collective-permute-start.1
  3.2 11.5 %collective-permute-start.2 = (f32[128,128]{1,0:T(8,128)S(1)}, f32[128,128]{1,0:T(8,128)S(1)}, u32[]{:S(2)}, u32[]{:S(2)}) collective-permute-start(f32[128,128]{1,0:T(8,128)S(1)} %broadcast_select_fusion.7), channel_id=1, source_target_pairs={{0,16},{1,17},{32,48},{33,49},{64,80},{65,81},{96,112},{97,113},{1... | collective-permute-start | bytes 196616 | tf_op jit(solution)/shard_map/diag_x/ppermute | solution.py:27
  4.9 20.3 %collective-permute-start.11 = (f32[3,128,128]{2,1,0:T(8,128)S(1)}, f32[3,128,128]{2,1,0:T(8,128)S(1)}, u32[]{:S(2)}, u32[]{:S(2)}) collective-permute-start(f32[3,128,128]{2,1,0:T(8,128)S(1)} %slice_bitcast_fusion), channel_id=1, source_target_pairs={{0,0},{1,33},{2,66},{3,99},{4,132},{5,165},{6,198},{7,231},{8,8},{... | collective-permute-start | bytes 589832 | tf_op jit(solution)/shard_map/rows/ppermute | solution.py:27
  13.1 27.7 %collective-permute-start.8 = (f32[3,128,128]{2,1,0:T(8,128)S(1)}, f32[3,128,128]{2,1,0:T(8,128)S(1)}, u32[]{:S(2)}, u32[]{:S(2)}) collective-permute-start(f32[3,128,128]{2,1,0:T(8,128)S(1)} %slice_bitcast_fusion), channel_id=1, source_target_pairs={{0,128},{1,129},{2,130},{3,131},{4,132},{5,133},{6,134},{7,135},{8... | collective-permute-start | bytes 589832 | tf_op jit(solution)/shard_map/cols/ppermute | solution.py:27
  14.8 11.1 %collective-permute-start.3 = (f32[128,128]{1,0:T(8,128)S(1)}, f32[128,128]{1,0:T(8,128)S(1)}, u32[]{:S(2)}, u32[]{:S(2)}) collective-permute-start(f32[128,128]{1,0:T(8,128)S(1)} %broadcast_select_fusion.8), channel_id=1, source_target_pairs={{0,8},{1,9},{16,24},{17,25},{32,40},{33,41},{48,56},{49,57},{64,72... | collective-permute-start | bytes 196616 | tf_op jit(solution)/shard_map/diag_x/ppermute | solution.py:27
  25.2 1.4 %collective-permute-start.12 = (f32[3,128,128]{2,1,0:T(8,128)S(1)}, f32[3,128,128]{2,1,0:T(8,128)S(1)}, u32[]{:S(2)}, u32[]{:S(2)}) collective-permute-start(f32[3,128,128]{2,1,0:T(8,128)S(1)} %collective-permute-done.11), channel_id=1, source_target_pairs={{0,4},{1,5},{8,12},{9,13},{16,20},{17,21},{24,28},{25,29},{32,36},... | collective-permute-start | bytes 589832 | tf_op jit(solution)/shard_map/rows/ppermute | solution.py:27
  25.9 2.0 %collective-permute-start.4 = (f32[128,128]{1,0:T(8,128)S(1)}, f32[128,128]{1,0:T(8,128)S(1)}, u32[]{:S(2)}, u32[]{:S(2)}) collective-permute-start(f32[128,128]{1,0:T(8,128)S(1)} %broadcast_select_fusion.9), channel_id=1, source_target_pairs={{0,4},{1,5},{8,12},{9,13},{16,20},{17,21},{24,28},{25,29},{32,36},... | collective-permute-start | bytes 196616 | tf_op jit(solution)/shard_map/diag_y/ppermute | solution.py:27
  26.6 14.0 %collective-permute-start.13 = (f32[3,128,128]{2,1,0:T(8,128)S(1)}, f32[3,128,128]{2,1,0:T(8,128)S(1)}, u32[]{:S(2)}, u32[]{:S(2)}) collective-permute-start(f32[3,128,128]{2,1,0:T(8,128)S(1)} %broadcast_select_fusion), channel_id=1, source_target_pairs={{0,2},{1,3},{4,6},{5,7},{8,10},{9,11},{12,14},{13,15},{16,18},{17,... | collective-permute-start | bytes 589832 | tf_op jit(solution)/shard_map/rows/ppermute | solution.py:27
  27.9 21.1 %collective-permute-start.5 = (f32[128,128]{1,0:T(8,128)S(1)}, f32[128,128]{1,0:T(8,128)S(1)}, u32[]{:S(2)}, u32[]{:S(2)}) collective-permute-start(f32[128,128]{1,0:T(8,128)S(1)} %broadcast_select_fusion.10), channel_id=1, source_target_pairs={{0,2},{1,3},{4,6},{5,7},{8,10},{9,11},{12,14},{13,15},{16,18},{17,... | collective-permute-start | bytes 196616 | tf_op jit(solution)/shard_map/diag_y/ppermute | solution.py:27
  40.7 8.4 %collective-permute-start.14 = (f32[3,128,128]{2,1,0:T(8,128)S(1)}, f32[3,128,128]{2,1,0:T(8,128)S(1)}, u32[]{:S(2)}, u32[]{:S(2)}) collective-permute-start(f32[3,128,128]{2,1,0:T(8,128)S(1)} %broadcast_select_fusion.1), channel_id=1, source_target_pairs={{0,8},{1,9},{2,10},{3,11},{4,12},{5,13},{6,14},{7,15},{8,16},{9,17... | collective-permute-start | bytes 589832 | tf_op jit(solution)/shard_map/rows/ppermute | solution.py:27
  40.8 16.9 %collective-permute-start.9 = (f32[3,128,128]{2,1,0:T(8,128)S(1)}, f32[3,128,128]{2,1,0:T(8,128)S(1)}, u32[]{:S(2)}, u32[]{:S(2)}) collective-permute-start(f32[3,128,128]{2,1,0:T(8,128)S(1)} %broadcast_select_fusion.2), channel_id=1, source_target_pairs={{0,64},{1,65},{2,66},{3,67},{4,68},{5,69},{6,70},{7,71},{8,72},{9,... | collective-permute-start | bytes 589832 | tf_op jit(solution)/shard_map/cols/ppermute | solution.py:27
  42.1 7.1 %collective-permute-start.16 = (f32[3,128,128]{2,1,0:T(8,128)S(1)}, f32[3,128,128]{2,1,0:T(8,128)S(1)}, u32[]{:S(2)}, u32[]{:S(2)}) collective-permute-start(f32[3,128,128]{2,1,0:T(8,128)S(1)} %broadcast_select_fusion.1), channel_id=1, source_target_pairs={{0,24},{1,25},{2,26},{3,27},{4,28},{5,29},{6,30},{7,31},{8,0},{9,1... | collective-permute-start | bytes 589832 | tf_op jit(solution)/shard_map/rows/ppermute | solution.py:27
  49.1 6.9 %collective-permute-start.15 = (f32[3,128,128]{2,1,0:T(8,128)S(1)}, f32[3,128,128]{2,1,0:T(8,128)S(1)}, u32[]{:S(2)}, u32[]{:S(2)}) collective-permute-start(f32[3,128,128]{2,1,0:T(8,128)S(1)} %collective-permute-done.14), channel_id=1, source_target_pairs={{0,8},{1,9},{2,10},{3,11},{4,12},{5,13},{6,14},{7,15},{8,16},{9,17... | collective-permute-start | bytes 589832 | tf_op jit(solution)/shard_map/rows/ppermute | solution.py:27
  49.1 7.0 %collective-permute-start.6 = (f32[128,128]{1,0:T(8,128)S(1)}, f32[128,128]{1,0:T(8,128)S(1)}, u32[]{:S(2)}, u32[]{:S(2)}) collective-permute-start(f32[128,128]{1,0:T(8,128)S(1)} %broadcast_select_fusion.11), channel_id=1, source_target_pairs={{0,1},{1,0},{2,3},{3,2},{4,5},{5,4},{6,7},{7,6},{8,9},{9,8},{10,11... | collective-permute-start | bytes 196616 | tf_op jit(solution)/shard_map/diag_swap/ppermute | solution.py:27
  56.0 9.1 %collective-permute-start.17 = (f32[4,3,128,128]{3,2,1,0:T(8,128)S(1)}, f32[4,3,128,128]{3,2,1,0:T(8,128)S(1)}, u32[]{:S(2)}, u32[]{:S(2)}) collective-permute-start(f32[4,3,128,128]{3,2,1,0:T(8,128)S(1)} %pad_maximum_fusion.near), channel_id=1, source_target_pairs={{0,1},{1,0},{2,3},{3,2},{4,5},{5,4},{6,7},{7,6},{8,9},{9,8},{10,11... | collective-permute-start | bytes 2359304 | tf_op jit(solution)/shard_map/rows/ppermute | solution.py:27
  56.1 4.6 %collective-permute-start.7 = (f32[128,128]{1,0:T(8,128)S(1)}, f32[128,128]{1,0:T(8,128)S(1)}, u32[]{:S(2)}, u32[]{:S(2)}) collective-permute-start(f32[128,128]{1,0:T(8,128)S(1)} %get-tuple-element.10), channel_id=1, source_target_pairs={{0,32},{1,33},{2,34},{3,35},{4,36},{5,37},{6,38},{7,39},{8,40},{9,... | collective-permute-start | bytes 196616 | tf_op jit(solution)/shard_map/diag_swap/ppermute | solution.py:27
  57.8 7.3 %collective-permute-start.10 = (f32[3,128,128]{2,1,0:T(8,128)S(1)}, f32[3,128,128]{2,1,0:T(8,128)S(1)}, u32[]{:S(2)}, u32[]{:S(2)}) collective-permute-start(f32[3,128,128]{2,1,0:T(8,128)S(1)} %broadcast_select_fusion.3), channel_id=1, source_target_pairs={{0,32},{1,33},{2,34},{3,35},{4,36},{5,37},{6,38},{7,39},{8,40},{9,... | collective-permute-start | bytes 589832 | tf_op jit(solution)/shard_map/cols/ppermute | solution.py:27

commit v2 on v0

v2 whole, which is shorter than its diff:
```python
import functools

import jax
import jax.numpy as jnp
from jax import lax
from jax.experimental import pallas as pl
from jax.experimental.pallas import tpu as pltpu
from jax.sharding import PartitionSpec as P

TB = 128
ROWS = 8
SIDE = 4
ROW_TILES = 12
COL_TILES = 3
QUARTER = 3
HIGHEST = lax.Precision.HIGHEST


def col_of(x, y, core):
    return (x * SIDE + y) * 2 + core


def device_of(z, col):
    return z * SIDE * SIDE * 2 + col


def send(value, pairs):
    return lax.ppermute(value, ("row", "col"), pairs)


def inverse_factor(tile):
    lane = lax.broadcasted_iota(jnp.int32, (8, TB), 1)
    sub = lax.broadcasted_iota(jnp.int32, (8, TB), 0)
    groups = TB // 8
    rows = [tile[8 * g : 8 * g + 8, :] for g in range(groups)]

    def across(value, k):
        return jnp.broadcast_to(value[:, k : k + 1], (8, TB))

    def down(value, k):
        return jnp.broadcast_to(value[k : k + 1, :], (8, TB))

    for p in range(groups):
        first = 8 * p
        wide = {g: [across(rows[g], first + k) for k in range(8)] for g in range(p, groups)}
        inside = (lane >= first) & (lane < first + 8)
        rows[p] = jnp.where(inside, jnp.where(lane - first == sub, 1.0, 0.0), rows[p])
        for g in range(p + 1, groups):
            rows[g] = jnp.where(inside, 0.0, rows[g])
        mine = wide[p]
        coef = {}
        scale = []
        top = []
        for k in range(8):
            r = lax.rsqrt(down(mine[k], k))
            scale.append(r)
            column = jnp.where(sub > k, mine[k] * r, 0.0)
            for m in range(k + 1, 8):
                coef[k, m] = down(mine[m], k) * r
                mine[m] = mine[m] - column * coef[k, m]
            u = down(rows[p], k) * r
            top.append(u)
            rows[p] = jnp.where(sub == k, u, rows[p] - column * u)
        for g in range(p + 1, groups):
            columns = []
            for k in range(8):
                value = wide[g][k]
                for m in range(k):
                    value = value - columns[m] * coef[m, k]
                columns.append(value * scale[k])
            total = rows[g]
            for k in range(8):
                total = total - columns[k] * top[k]
            rows[g] = total
    return jnp.concatenate([jnp.where(lane <= sub + 8 * g, rows[g], 0.0) for g in range(groups)], axis=0)


def halves(value):
    high = value.astype(jnp.bfloat16)
    return high, (value - high.astype(jnp.float32)).astype(jnp.bfloat16)


def product(a, b, transposed):
    dims = (((1,), (1 if transposed else 0,)), ((), ()))
    dot = functools.partial(lax.dot_general, dimension_numbers=dims, preferred_element_type=jnp.float32)
    return dot(a[0], b[0]) + (dot(a[0], b[1]) + dot(a[1], b[0]))


def exact(a, b, transposed=False):
    dims = (((1,), (1 if transposed else 0,)), ((), ()))
    return lax.dot_general(a, b, dims, precision=HIGHEST, preferred_element_type=jnp.float32)


def first_block(place, own, by_core, by_row, by_both, inv00, mixed, schur):
    odd_row = lax.rem(place[0], 2) == 1
    odd_col = lax.rem(place[1], 2) == 1
    near_row = jnp.where(odd_col, by_core[...], own[...])
    far_row = jnp.where(odd_col, by_both[...], by_row[...])
    near_row_other = jnp.where(odd_col, own[...], by_core[...])
    far_row_other = jnp.where(odd_col, by_row[...], by_both[...])
    a00 = jnp.where(odd_row, far_row, near_row)
    a10 = jnp.where(odd_row, near_row, far_row)
    a11 = jnp.where(odd_row, near_row_other, far_row_other)
    inv = inverse_factor(a00)
    l10 = exact(a10, inv, transposed=True)
    schur[...] = a11 - exact(l10, l10, transposed=True)
    mixed[...] = exact(l10, inv)
    inv00[...] = inv


def second_block(inv00, mixed, schur, high, low):
    inv11 = inverse_factor(schur[...])
    inv10 = -exact(inv11, mixed[...])
    zero = jnp.zeros((TB, TB), jnp.float32)
    for i, line in enumerate(((inv00[...], zero), (inv10, inv11))):
        for j, value in enumerate(line):
            part = slice(i * TB, (i + 1) * TB), slice(j * TB, (j + 1) * TB)
            high[part], low[part] = halves(value)


def update(place, high, low, part, other_part, near, far, kernel, out, block, sem, sems):
    my_row, my_col = place[0], place[1]
    load = pltpu.make_async_copy(kernel, block, sem)
    load.start()
    odd_row = lax.rem(my_row, 2) == 1
    my_x = my_col // (2 * SIDE)
    my_y = lax.rem(my_col // 2, SIDE)
    swapped = lax.rem(my_col, 2) == 1
    inv = high[...], low[...]
    top = jnp.concatenate(
        [
            jnp.concatenate([jnp.where(odd_row, other_part[t], part[t]) for t in range(COL_TILES)], axis=1),
            jnp.concatenate([jnp.where(odd_row, part[t], other_part[t]) for t in range(COL_TILES)], axis=1),
        ],
        axis=0,
    )
    right = halves(product(inv, halves(top), False))
    lane = lax.broadcasted_iota(jnp.int32, (TB, TB), 1)
    sub = lax.broadcasted_iota(jnp.int32, (TB, TB), 0)

    load.wait()
    for quarter in range(SIDE):
        from_x = lax.rem(my_x - quarter + SIDE, SIDE)
        from_y = lax.rem(my_y - quarter + SIDE, SIDE)
        zero = jnp.where(swapped, far[from_x], near[from_x]).reshape(QUARTER * TB, TB)
        one = jnp.where(swapped, near[from_y], far[from_y]).reshape(QUARTER * TB, TB)
        left = product(halves(jnp.concatenate([zero, one], axis=1)), inv, True)
        change = product(halves(left), right, False)
        for i in range(QUARTER):
            s = quarter * QUARTER + i
            rows = slice(i * TB, (i + 1) * TB)
            for t in range(COL_TILES):
                block[s, t] = block[s, t] - change[rows, t * TB : (t + 1) * TB]

            @pl.when(my_col == 0)
            def _():
                block[s, 0] = left[rows, :TB]

            @pl.when(my_col == 1)
            def _():
                block[s, 0] = left[rows, TB:]

            if s == 0:

                @pl.when(my_row < 2)
                def _():
                    for t in range(1, COL_TILES):
                        block[0, t] = jnp.zeros((TB, TB), jnp.float32)

                    @pl.when((my_col > 1) | (my_row < my_col))
                    def _():
                        block[0, 0] = jnp.zeros((TB, TB), jnp.float32)

                    @pl.when(my_row == my_col)
                    def _():
                        block[0, 0] = jnp.where(lane <= sub, block[0, 0], 0.0)

            pltpu.make_async_copy(block.at[s], out.at[s], sems.at[s]).start()
    for s in range(ROW_TILES):
        pltpu.make_async_copy(block.at[s], out.at[s], sems.at[s]).wait()


def after(value, *others):
    return lax.optimization_barrier((value, *others))[0]


def shards(kernel):
    my_row = lax.axis_index("row").astype(jnp.int32)
    my_col = lax.axis_index("col").astype(jnp.int32)
    my_x = my_col // (2 * SIDE)
    my_y = (my_col // 2) % SIDE
    my_core = my_col % 2
    tiles = kernel.transpose(0, 2, 1, 3)
    place = jnp.stack([my_row, my_col])

    zs = range(ROWS)
    sides = range(SIDE)
    cores = range(2)
    cols = range(2 * SIDE * SIDE)

    def at(z, u, v, core):
        return device_of(z, col_of(u, v, core) if core == 0 else col_of(v, u, core))

    def plane_pairs(planes, us, vs, du, dv):
        return [
            (at(z, u, v, c), at(z, (u + du) % SIDE, (v + dv) % SIDE, c)) for z in planes for u in us for v in vs for c in cores
        ]

    def z_pairs(planes, step, columns):
        return [(device_of(z, c), device_of(z + step, c)) for z in planes for c in columns]

    my_u = jnp.where(my_core == 0, my_x, my_y)
    my_v = jnp.where(my_core == 0, my_y, my_x)
    swap_core = [(device_of(z, c), device_of(z, c ^ 1)) for z in zs for c in cols]
    swap_row = [(device_of(z, c), device_of(z ^ 1, c)) for z in zs for c in cols]
    swap_both = [(device_of(z, c), device_of(z ^ 1, c ^ 1)) for z in zs for c in cols]
    low_planes = (0, 1)

    column = tiles[:, 0].reshape(SIDE, QUARTER, TB, TB)
    head = tiles[0]
    diag = lax.optimization_barrier((head[0], column))[0]
    got = send(diag, plane_pairs(low_planes, (0,), (0,), 2, 0))
    quarter1 = send(column[1], plane_pairs(zs, (0,), (0,), 1, 0))
    quarter3 = send(column[3], plane_pairs(zs, (0,), (0,), 3, 0))
    diag1 = jnp.where(my_u == 2, got, diag)

    got = send(diag1, plane_pairs(low_planes, (0, 2), (0,), 1, 0))
    quarter2 = send(after(column[2], diag1), plane_pairs(zs, (0,), (0,), 2, 0))
    part = after(head, diag1)
    part_got = send(part, z_pairs(low_planes, 4, cols))
    diag2 = jnp.where(my_u % 2 == 1, got, diag1)

    got = send(diag2, plane_pairs(low_planes, sides, (0,), 0, 2))
    diag3 = jnp.where(my_v == 2, got, diag2)

    got = send(diag3, plane_pairs(low_planes, sides, (0, 2), 0, 1))
    quarter1, quarter2, quarter3 = (after(q, diag3) for q in (quarter1, quarter2, quarter3))
    piece = jnp.where(my_u == 0, column[0], jnp.where(my_u == 1, quarter1, jnp.where(my_u == 2, quarter2, quarter3)))
    piece1 = send(piece, plane_pairs(zs, sides, (0,), 0, 1))
    diag4 = jnp.where(my_v % 2 == 1, got, diag3)

    got = send(diag4, z_pairs(low_planes, 4, cols))
    piece3 = send(after(piece, diag4), plane_pairs(zs, sides, (0,), 0, 3))
    piece2 = send(after(piece, diag4), plane_pairs(zs, sides, (0,), 0, 2))
    diag5 = jnp.where((my_row == 4) | (my_row == 5), got, diag4)

    got = send(diag5, z_pairs((0, 1, 4, 5), 2, cols))
    part = jnp.where((my_row == 4) | (my_row == 5), after(part_got, diag5), part)
    part_got = send(part, z_pairs((0, 1, 4, 5), 2, cols))
    diag6 = jnp.where(my_row % 4 >= 2, got, diag5)

    by_core, by_row, by_both = send(diag6, swap_core), send(diag6, swap_row), send(diag6, swap_both)
    piece1, piece2, piece3 = (after(q, by_row) for q in (piece1, piece2, piece3))
    piece = jnp.where(my_v == 0, piece, jnp.where(my_v == 1, piece1, jnp.where(my_v == 2, piece2, piece3)))
    across = send(piece, plane_pairs(zs, sides, sides, 2, 0))
    up = send(piece, plane_pairs(zs, sides, sides, 1, 0))
    down = send(piece, plane_pairs(zs, sides, sides, 3, 0))

    part = jnp.where(my_row % 4 >= 2, part_got, part)
    other_part = send(part, swap_row)
    diag6 = after(diag6, part)

    vmem = pl.BlockSpec(memory_space=pltpu.VMEM)
    smem = pl.BlockSpec(memory_space=pltpu.SMEM)
    anywhere = pl.BlockSpec(memory_space=pl.ANY)
    tile = jax.ShapeDtypeStruct((TB, TB), jnp.float32)
    inverse = jax.ShapeDtypeStruct((2 * TB, 2 * TB), jnp.bfloat16)
    inv00, mixed, schur = pl.pallas_call(
        first_block,
        out_shape=[tile] * 3,
        in_specs=[smem] + [vmem] * 4,
        out_specs=[vmem] * 3,
        compiler_params=pltpu.CompilerParams(vmem_limit_bytes=8 * 1024 * 1024),
        name="first_block",
    )(place, diag6, by_core, by_row, by_both)

    up, down, across = (after(q, schur) for q in (up, down, across))
    near = jnp.stack([piece, up, across, down])
    far = send(near, swap_core)
    high, low = pl.pallas_call(
        second_block,
        out_shape=[inverse] * 2,
        in_specs=[vmem] * 3,
        out_specs=[vmem] * 2,
        compiler_params=pltpu.CompilerParams(vmem_limit_bytes=8 * 1024 * 1024),
        name="second_block",
    )(inv00, mixed, schur)

    far, other_part = (after(q, high) for q in (far, other_part))
    result = pl.pallas_call(
        update,
        out_shape=jax.ShapeDtypeStruct(tiles.shape, tiles.dtype),
        in_specs=[smem] + [vmem] * 6 + [anywhere],
        out_specs=anywhere,
        scratch_shapes=[
            pltpu.VMEM((ROW_TILES, COL_TILES, TB, TB), jnp.float32),
            pltpu.SemaphoreType.DMA,
            pltpu.SemaphoreType.DMA((ROW_TILES,)),
        ],
        compiler_params=pltpu.CompilerParams(vmem_limit_bytes=24 * 1024 * 1024),
        name="update",
    )(place, high, low, part, other_part, near, far, tiles)
    return result.transpose(0, 2, 1, 3)


def solution(mesh):
    return jax.shard_map(
        shards,
        mesh=mesh,
        in_specs=(P(None, "row", None, "col"),),
        out_specs=P(None, "row", None, "col"),
        check_vma=False,
    )
```

time: 649 us -> 69.7 us (0.11)
  the two profiles are of different devices: /device:TPU:200 before, /device:TPU:1 now
where the time goes in v2:
time: 69.7 us; the launch traced here: 69.3 us
  starting transfers between devices  45.3 us (65%)
  Pallas kernels  15.5 us (22%)
  waiting for transfers between devices  4.49 us (6%)
  local copies, waits for them, and re-layouts  3.1 us (4%)
    ppermute x22, starting transfers between devices, send(): return lax.ppermute(value, ('row', 'col'), pairs)  45.3 us
    pallas_call x1, Pallas kernels, shards(): pl.pallas_call(update, out_shape=jax.ShapeDtypeStruct(tiles.shape, tiles....  6.12 us
    pallas_call x1, Pallas kernels, shards(): pl.pallas_call(first_block, out_shape=[tile] * 3, in_specs=[smem] + [vmem...  5.3 us
    ppermute x22, waiting for transfers between devices, send(): return lax.ppermute(value, ('row', 'col'), pairs)  4.49 us
    pallas_call x1, Pallas kernels, shards(): pl.pallas_call(second_block, out_shape=[inverse] * 2, in_specs=[vmem] * 3...  4.08 us
  transfers between devices with their start and end apart: 22, of which 5 were waited for; matrix products, arithmetic and copies ran while one was open for 3% of the time, Pallas kernels for 14%

profile of v2, /device:TPU:1, one launch (start us, length us, event | category | flops | bytes accessed | tf_op | source)
XLA Modules:
  0.0 69.3 jit_solution(11483019875567813111)
XLA Ops:
  0.0 1.0 %slice_bitcast_fusion.5 = f32[128,128]{1,0:T(8,128)S(1)} fusion(f32[12,3,128,128]{3,2,1,0:T(8,128)} %bitcast.28), kind=kLoop, calls=%fused_computation.10 | loop fusion | bytes 131072 | tf_op jit(solution)/shard_map/squeeze | solution.py:221
  1.0 5.6 %collective-permute-start = (f32[128,128]{1,0:T(8,128)S(1)}, f32[128,128]{1,0:T(8,128)S(1)}, u32[]{:S(2)}, u32[]{:S(2)}) collective-permute-start(f32[128,128]{1,0:T(8,128)S(1)} %slice_bitcast_fusion.5), channel_id=1, source_target_pairs={{0,16},{1,5},{32,48},{33,37}} | collective-permute-start | bytes 196616 | tf_op jit(solution)/shard_map/ppermute | solution.py:28
  6.7 1.3 %collective-permute-done = f32[128,128]{1,0:T(8,128)S(1)} collective-permute-done((f32[128,128]{1,0:T(8,128)S(1)}, f32[128,128]{1,0:T(8,128)S(1)}, u32[]{:S(2)}, u32[]{:S(2)}) %collective-permute-start) | collective-permute-done | bytes 65568 | tf_op jit(solution)/shard_map/ppermute | solution.py:28
  8.0 1.3 %collective-permute-start.1 = (f32[128,128]{1,0:T(8,128)S(1)}, f32[128,128]{1,0:T(8,128)S(1)}, u32[]{:S(2)}, u32[]{:S(2)}) collective-permute-start(f32[128,128]{1,0:T(8,128)S(1)} %broadcast_select_fusion.2), channel_id=1, source_target_pairs={{0,8},{1,3},{16,24},{5,7},{32,40},{33,35},{48,56},{37,39}} | collective-permute-start | bytes 196616 | tf_op jit(solution)/shard_map/ppermute | solution.py:28
  9.3 1.3 %collective-permute-done.1 = f32[128,128]{1,0:T(8,128)S(1)} collective-permute-done((f32[128,128]{1,0:T(8,128)S(1)}, f32[128,128]{1,0:T(8,128)S(1)}, u32[]{:S(2)}, u32[]{:S(2)}) %collective-permute-start.1) | collective-permute-done | bytes 65568 | tf_op jit(solution)/shard_map/ppermute | solution.py:28
  10.6 1.3 %collective-permute-start.2 = (f32[128,128]{1,0:T(8,128)S(1)}, f32[128,128]{1,0:T(8,128)S(1)}, u32[]{:S(2)}, u32[]{:S(2)}) collective-permute-start(f32[128,128]{1,0:T(8,128)S(1)} %broadcast_select_fusion.3), channel_id=1, source_target_pairs={{0,4},{1,17},{8,12},{3,19},{16,20},{5,21},{24,28},{7,23},{32,36},{... | collective-permute-start | bytes 196616 | tf_op jit(solution)/shard_map/ppermute | solution.py:28
  11.9 1.2 %slice_bitcast_fusion = (f32[3,128,128]{2,1,0:T(8,128)S(1)}, f32[3,128,128]{2,1,0:T(8,128)S(1)}, f32[3,128,128]{2,1,0:T(8,128)S(1)}) fusion(f32[12,3,128,128]{3,2,1,0:T(8,128)} %bitcast.29), kind=kLoop, calls=%fused_computation.1 | loop fusion | bytes 1179648 | tf_op jit(solution)/shard_map/squeeze | solution.py:224
  13.1 5.8 %collective-permute-start.14 = (f32[3,128,128]{2,1,0:T(8,128)S(1)}, f32[3,128,128]{2,1,0:T(8,128)S(1)}, u32[]{:S(2)}, u32[]{:S(2)}) collective-permute-start(f32[3,128,128]{2,1,0:T(8,128)S(1)} %get-tuple-element.47), channel_id=1, source_target_pairs={{0,24},{1,7},{32,56},{33,39},{64,88},{65,71},{96,120},{97,103},{12... | collective-permute-start | bytes 589832 | tf_op jit(solution)/shard_map/ppermute | solution.py:28
  18.9 2.0 %collective-permute-start.12 = (f32[3,128,128]{2,1,0:T(8,128)S(1)}, f32[3,128,128]{2,1,0:T(8,128)}, u32[]{:S(2)}, u32[]{:S(2)}) collective-permute-start(f32[3,128,128]{2,1,0:T(8,128)S(1)} %get-tuple-element.48), channel_id=1, source_target_pairs={{0,8},{1,3},{32,40},{33,35},{64,72},{65,67},{96,104},{97,99},{128,... | collective-permute-start | bytes 589832 | tf_op jit(solution)/shard_map/ppermute | solution.py:28
  20.9 1.3 %collective-permute-start.3 = (f32[128,128]{1,0:T(8,128)S(1)}, f32[128,128]{1,0:T(8,128)S(1)}, u32[]{:S(2)}, u32[]{:S(2)}) collective-permute-start(f32[128,128]{1,0:T(8,128)S(1)} %broadcast_select_fusion.4), channel_id=1, source_target_pairs={{0,2},{1,9},{4,6},{17,25},{8,10},{3,11},{12,14},{19,27},{16,18},{5... | collective-permute-start | bytes 196616 | tf_op jit(solution)/shard_map/ppermute | solution.py:28
  22.2 0.9 %slice_bitcast_fusion.4 = f32[3,128,128]{2,1,0:T(8,128)S(1)} fusion(f32[12,3,128,128]{3,2,1,0:T(8,128)} %bitcast.30), kind=kLoop, calls=%fused_computation.6 | loop fusion | bytes 393216 | tf_op jit(solution)/shard_map/squeeze | solution.py:220
  23.2 1.3 %collective-permute-start.13 = (f32[3,128,128]{2,1,0:T(8,128)S(1)}, f32[3,128,128]{2,1,0:T(8,128)S(1)}, u32[]{:S(2)}, u32[]{:S(2)}) collective-permute-start(f32[3,128,128]{2,1,0:T(8,128)S(1)} %get-tuple-element.36), channel_id=1, source_target_pairs={{0,16},{1,5},{32,48},{33,37},{64,80},{65,69},{96,112},{97,101},{12... | collective-permute-start | bytes 589832 | tf_op jit(solution)/shard_map/ppermute | solution.py:28
  24.5 1.3 %collective-permute-start.4 = (f32[128,128]{1,0:T(8,128)S(1)}, f32[128,128]{1,0:T(8,128)S(1)}, u32[]{:S(2)}, u32[]{:S(2)}) collective-permute-start(f32[128,128]{1,0:T(8,128)S(1)} %broadcast_select_fusion.5), channel_id=1, source_target_pairs={{0,128},{1,129},{2,130},{3,131},{4,132},{5,133},{6,134},{7,135},{8... | collective-permute-start | bytes 196616 | tf_op jit(solution)/shard_map/ppermute | solution.py:28
  25.8 0.1 pad_add_fusion.place
  25.9 1.3 %collective-permute-start.6 = (f32[3,128,128]{2,1,0:T(8,128)S(1)}, f32[3,128,128]{2,1,0:T(8,128)S(1)}, u32[]{:S(2)}, u32[]{:S(2)}) collective-permute-start(f32[3,128,128]{2,1,0:T(8,128)S(1)} %slice_bitcast_fusion.4), channel_id=1, source_target_pairs={{0,128},{1,129},{2,130},{3,131},{4,132},{5,133},{6,134},{7,135},{8... | collective-permute-start | bytes 589832 | tf_op jit(solution)/shard_map/ppermute | solution.py:28
  27.2 0.6 collective-permute-done.13
  27.8 1.3 %collective-permute-start.5 = (f32[128,128]{1,0:T(8,128)S(1)}, f32[128,128]{1,0:T(8,128)S(1)}, u32[]{:S(2)}, u32[]{:S(2)}) collective-permute-start(f32[128,128]{1,0:T(8,128)S(1)} %broadcast_select_fusion.6), channel_id=1, source_target_pairs={{0,64},{1,65},{2,66},{3,67},{4,68},{5,69},{6,70},{7,71},{8,72},{9,... | collective-permute-start | bytes 196616 | tf_op jit(solution)/shard_map/ppermute | solution.py:28
  29.2 1.3 %collective-permute-start.17 = (f32[3,128,128]{2,1,0:T(8,128)S(1)}, f32[3,128,128]{2,1,0:T(8,128)S(1)}, u32[]{:S(2)}, u32[]{:S(2)}) collective-permute-start(f32[3,128,128]{2,1,0:T(8,128)S(1)} %fusion), channel_id=1, source_target_pairs={{0,6},{1,25},{8,14},{3,27},{16,22},{5,29},{24,30},{7,31},{32,38},{... | collective-permute-start | bytes 589832 | tf_op jit(solution)/shard_map/ppermute | solution.py:28
  30.5 1.3 %collective-permute-start.16 = (f32[3,128,128]{2,1,0:T(8,128)S(1)}, f32[3,128,128]{2,1,0:T(8,128)S(1)}, u32[]{:S(2)}, u32[]{:S(2)}) collective-permute-start(f32[3,128,128]{2,1,0:T(8,128)S(1)} %fusion), channel_id=1, source_target_pairs={{0,4},{1,17},{8,12},{3,19},{16,20},{5,21},{24,28},{7,23},{32,36},{... | collective-permute-start | bytes 589832 | tf_op jit(solution)/shard_map/ppermute | solution.py:28
  31.8 1.4 %collective-permute-start.15 = (f32[3,128,128]{2,1,0:T(8,128)S(1)}, f32[3,128,128]{2,1,0:T(8,128)S(1)}, u32[]{:S(2)}, u32[]{:S(2)}) collective-permute-start(f32[3,128,128]{2,1,0:T(8,128)S(1)} %fusion), channel_id=1, source_target_pairs={{0,2},{1,9},{8,10},{3,11},{16,18},{5,13},{24,26},{7,15},{32,34},{3... | collective-permute-start | bytes 589832 | tf_op jit(solution)/shard_map/ppermute | solution.py:28
  33.2 3.3 %collective-permute-start.9 = (f32[128,128]{1,0:T(8,128)S(1)}, f32[128,128]{1,0:T(8,128)S(1)}, u32[]{:S(2)}, u32[]{:S(2)}) collective-permute-start(f32[128,128]{1,0:T(8,128)S(1)} %broadcast_select_fusion.7.own), channel_id=1, source_target_pairs={{0,32},{1,33},{2,34},{3,35},{4,36},{5,37},{6,38},{7,39},{8,40},{9,... | collective-permute-start | bytes 196616 | tf_op jit(solution)/shard_map/ppermute | solution.py:28
  36.6 5.0 %collective-permute-start.7 = (f32[3,128,128]{2,1,0:T(8,128)S(1)}, f32[3,128,128]{2,1,0:T(8,128)S(1)}, u32[]{:S(2)}, u32[]{:S(2)}) collective-permute-start(f32[3,128,128]{2,1,0:T(8,128)S(1)} %broadcast_select_fusion), channel_id=1, source_target_pairs={{0,64},{1,65},{2,66},{3,67},{4,68},{5,69},{6,70},{7,71},{8,72},{9,... | collective-permute-start | bytes 589832 | tf_op jit(solution)/shard_map/ppermute | solution.py:28
  41.6 2.5 %collective-permute-start.10 = (f32[128,128]{1,0:T(8,128)S(1)}, f32[128,128]{1,0:T(8,128)S(1)}, u32[]{:S(2)}, u32[]{:S(2)}) collective-permute-start(f32[128,128]{1,0:T(8,128)S(1)} %broadcast_select_fusion.7.own), channel_id=1, source_target_pairs={{0,33},{1,32},{2,35},{3,34},{4,37},{5,36},{6,39},{7,38},{8,41},{9,... | collective-permute-start | bytes 196616 | tf_op jit(solution)/shard_map/ppermute | solution.py:28
  44.1 0.1 collective-permute-start.20
  44.2 5.3 %collective-permute-start.19 = (f32[3,128,128]{2,1,0:T(8,128)S(1)}, f32[3,128,128]{2,1,0:T(8,128)S(1)}, u32[]{:S(2)}, u32[]{:S(2)}) collective-permute-start(f32[3,128,128]{2,1,0:T(8,128)S(1)} %select_select_fusion), channel_id=1, source_target_pairs={{0,16},{1,5},{2,18},{9,13},{4,20},{17,21},{6,22},{25,29},{8,24},{3... | collective-permute-start | bytes 589832 | tf_op jit(solution)/shard_map/ppermute | solution.py:28
  49.6 5.3 %first_block.1 = (f32[128,128]{1,0:T(8,128)S(1)}, f32[128,128]{1,0:T(8,128)S(1)}, f32[128,128]{1,0:T(8,128)S(1)}) custom-call(s32[2]{0:T(128)S(1)} %pad_add_fusion.place, f32[128,128]{1,0:T(8,128)S(1)} %broadcast_select_fusion.7.own, f32[128,128]{1,0:T(8,128)S(1)} %collective-permute-done.8.by_core, f32[128,128]{1,0:T(8,128)S(1)} %collective-permute-done.9.by_row, ...), custom_call_target="tpu_custom_call" | custom-call | tf_op jit(solution)/shard_map/first_block/pallas_call | solution.py:268
  54.9 0.4 collective-permute-done.18
  55.3 0.1 collective-permute-start.21
  55.4 2.5 %collective-permute-start.11 = (f32[3,128,128]{2,1,0:T(8,128)S(1)}, f32[3,128,128]{2,1,0:T(8,128)S(1)}, u32[]{:S(2)}, u32[]{:S(2)}) collective-permute-start(f32[3,128,128]{2,1,0:T(8,128)S(1)} %broadcast_select_fusion.1.part), channel_id=1, source_target_pairs={{0,32},{1,33},{2,34},{3,35},{4,36},{5,37},{6,38},{7,39},{8,40},{9,... | collective-permute-start | bytes 589832 | tf_op jit(solution)/shard_map/ppermute | solution.py:28
  58.0 4.1 %second_block.1 = (bf16[256,256]{1,0:T(8,128)(2,1)S(1)}, bf16[256,256]{1,0:T(8,128)(2,1)S(1)}) custom-call(f32[128,128]{1,0:T(8,128)S(1)} %get-tuple-element.29.inv00, f32[128,128]{1,0:T(8,128)S(1)} %get-tuple-element.30.mixed, f32[128,128]{1,0:T(8,128)S(1)} %get-tuple-element.31.schur), custom_call_target="tpu_custom_call" | custom-call | tf_op jit(solution)/shard_map/second_block/pallas_call | solution.py:280
  62.1 1.0 %collective-permute-done.11.other_part = f32[3,128,128]{2,1,0:T(8,128)S(1)} collective-permute-done((f32[3,128,128]{2,1,0:T(8,128)S(1)}, f32[3,128,128]{2,1,0:T(8,128)S(1)}, u32[]{:S(2)}, u32[]{:S(2)}) %collective-permute-start.11) | collective-permute-done | bytes 196640 | tf_op jit(solution)/shard_map/ppermute | solution.py:28
  63.0 6.1 %update.1 = f32[12,3,128,128]{3,2,1,0:T(8,128)} custom-call(s32[2]{0:T(128)S(1)} %pad_add_fusion.place, bf16[256,256]{1,0:T(8,128)(2,1)S(1)} %get-tuple-element.32.high, bf16[256,256]{1,0:T(8,128)(2,1)S(1)} %get-tuple-element.33.low, f32[3,128,128]{2,1,0:T(8,128)S(1)} %broadcast_select_fusion.1.part, f32[3,128,128]{2,1,0:T(8,128)S(1)} %collective-permute-done.11.other_part, ...), custom_call_target="tpu_custom_call" | custom-call | tf_op jit(solution)/shard_map/update/pallas_call | solution.py:290
  (32 shorter events, 0.3 us)
Async XLA Ops:
  0.0 29.1 %copy-start = (f32[12,128,3,128]{3,1,2,0:T(8,128)S(1)}, f32[12,128,3,128]{3,1,2,0:T(8,128)}, u32[]{:S(2)}) copy-start(f32[12,128,3,128]{3,1,2,0:T(8,128)} %param.1) | copy-start | bytes 7077892
  1.0 7.0 %collective-permute-start = (f32[128,128]{1,0:T(8,128)S(1)}, f32[128,128]{1,0:T(8,128)S(1)}, u32[]{:S(2)}, u32[]{:S(2)}) collective-permute-start(f32[128,128]{1,0:T(8,128)S(1)} %slice_bitcast_fusion.5), channel_id=1, source_target_pairs={{0,16},{1,5},{32,48},{33,37}} | collective-permute-start | bytes 196616 | tf_op jit(solution)/shard_map/ppermute | solution.py:28
  8.0 2.6 %collective-permute-start.1 = (f32[128,128]{1,0:T(8,128)S(1)}, f32[128,128]{1,0:T(8,128)S(1)}, u32[]{:S(2)}, u32[]{:S(2)}) collective-permute-start(f32[128,128]{1,0:T(8,128)S(1)} %broadcast_select_fusion.2), channel_id=1, source_target_pairs={{0,8},{1,3},{16,24},{5,7},{32,40},{33,35},{48,56},{37,39}} | collective-permute-start | bytes 196616 | tf_op jit(solution)/shard_map/ppermute | solution.py:28
  10.6 10.3 %collective-permute-start.2 = (f32[128,128]{1,0:T(8,128)S(1)}, f32[128,128]{1,0:T(8,128)S(1)}, u32[]{:S(2)}, u32[]{:S(2)}) collective-permute-start(f32[128,128]{1,0:T(8,128)S(1)} %broadcast_select_fusion.3), channel_id=1, source_target_pairs={{0,4},{1,17},{8,12},{3,19},{16,20},{5,21},{24,28},{7,23},{32,36},{... | collective-permute-start | bytes 196616 | tf_op jit(solution)/shard_map/ppermute | solution.py:28
  13.1 14.1 %collective-permute-start.14 = (f32[3,128,128]{2,1,0:T(8,128)S(1)}, f32[3,128,128]{2,1,0:T(8,128)S(1)}, u32[]{:S(2)}, u32[]{:S(2)}) collective-permute-start(f32[3,128,128]{2,1,0:T(8,128)S(1)} %get-tuple-element.47), channel_id=1, source_target_pairs={{0,24},{1,7},{32,56},{33,39},{64,88},{65,71},{96,120},{97,103},{12... | collective-permute-start | bytes 589832 | tf_op jit(solution)/shard_map/ppermute | solution.py:28
  18.9 8.3 %collective-permute-start.12 = (f32[3,128,128]{2,1,0:T(8,128)S(1)}, f32[3,128,128]{2,1,0:T(8,128)}, u32[]{:S(2)}, u32[]{:S(2)}) collective-permute-start(f32[3,128,128]{2,1,0:T(8,128)S(1)} %get-tuple-element.48), channel_id=1, source_target_pairs={{0,8},{1,3},{32,40},{33,35},{64,72},{65,67},{96,104},{97,99},{128,... | collective-permute-start | bytes 589832 | tf_op jit(solution)/shard_map/ppermute | solution.py:28
  20.9 3.6 %collective-permute-start.3 = (f32[128,128]{1,0:T(8,128)S(1)}, f32[128,128]{1,0:T(8,128)S(1)}, u32[]{:S(2)}, u32[]{:S(2)}) collective-permute-start(f32[128,128]{1,0:T(8,128)S(1)} %broadcast_select_fusion.4), channel_id=1, source_target_pairs={{0,2},{1,9},{4,6},{17,25},{8,10},{3,11},{12,14},{19,27},{16,18},{5... | collective-permute-start | bytes 196616 | tf_op jit(solution)/shard_map/ppermute | solution.py:28
  23.2 4.6 %collective-permute-start.13 = (f32[3,128,128]{2,1,0:T(8,128)S(1)}, f32[3,128,128]{2,1,0:T(8,128)S(1)}, u32[]{:S(2)}, u32[]{:S(2)}) collective-permute-start(f32[3,128,128]{2,1,0:T(8,128)S(1)} %get-tuple-element.36), channel_id=1, source_target_pairs={{0,16},{1,5},{32,48},{33,37},{64,80},{65,69},{96,112},{97,101},{12... | collective-permute-start | bytes 589832 | tf_op jit(solution)/shard_map/ppermute | solution.py:28
  24.5 3.3 %collective-permute-start.4 = (f32[128,128]{1,0:T(8,128)S(1)}, f32[128,128]{1,0:T(8,128)S(1)}, u32[]{:S(2)}, u32[]{:S(2)}) collective-permute-start(f32[128,128]{1,0:T(8,128)S(1)} %broadcast_select_fusion.5), channel_id=1, source_target_pairs={{0,128},{1,129},{2,130},{3,131},{4,132},{5,133},{6,134},{7,135},{8... | collective-permute-start | bytes 196616 | tf_op jit(solution)/shard_map/ppermute | solution.py:28
  25.9 7.3 %collective-permute-start.6 = (f32[3,128,128]{2,1,0:T(8,128)S(1)}, f32[3,128,128]{2,1,0:T(8,128)S(1)}, u32[]{:S(2)}, u32[]{:S(2)}) collective-permute-start(f32[3,128,128]{2,1,0:T(8,128)S(1)} %slice_bitcast_fusion.4), channel_id=1, source_target_pairs={{0,128},{1,129},{2,130},{3,131},{4,132},{5,133},{6,134},{7,135},{8... | collective-permute-start | bytes 589832 | tf_op jit(solution)/shard_map/ppermute | solution.py:28
  27.8 5.4 %collective-permute-start.5 = (f32[128,128]{1,0:T(8,128)S(1)}, f32[128,128]{1,0:T(8,128)S(1)}, u32[]{:S(2)}, u32[]{:S(2)}) collective-permute-start(f32[128,128]{1,0:T(8,128)S(1)} %broadcast_select_fusion.6), channel_id=1, source_target_pairs={{0,64},{1,65},{2,66},{3,67},{4,68},{5,69},{6,70},{7,71},{8,72},{9,... | collective-permute-start | bytes 196616 | tf_op jit(solution)/shard_map/ppermute | solution.py:28
  29.2 14.9 %collective-permute-start.17 = (f32[3,128,128]{2,1,0:T(8,128)S(1)}, f32[3,128,128]{2,1,0:T(8,128)S(1)}, u32[]{:S(2)}, u32[]{:S(2)}) collective-permute-start(f32[3,128,128]{2,1,0:T(8,128)S(1)} %fusion), channel_id=1, source_target_pairs={{0,6},{1,25},{8,14},{3,27},{16,22},{5,29},{24,30},{7,31},{32,38},{... | collective-permute-start | bytes 589832 | tf_op jit(solution)/shard_map/ppermute | solution.py:28
  30.5 13.6 %collective-permute-start.16 = (f32[3,128,128]{2,1,0:T(8,128)S(1)}, f32[3,128,128]{2,1,0:T(8,128)S(1)}, u32[]{:S(2)}, u32[]{:S(2)}) collective-permute-start(f32[3,128,128]{2,1,0:T(8,128)S(1)} %fusion), channel_id=1, source_target_pairs={{0,4},{1,17},{8,12},{3,19},{16,20},{5,21},{24,28},{7,23},{32,36},{... | collective-permute-start | bytes 589832 | tf_op jit(solution)/shard_map/ppermute | solution.py:28
  31.8 12.3 %collective-permute-start.15 = (f32[3,128,128]{2,1,0:T(8,128)S(1)}, f32[3,128,128]{2,1,0:T(8,128)S(1)}, u32[]{:S(2)}, u32[]{:S(2)}) collective-permute-start(f32[3,128,128]{2,1,0:T(8,128)S(1)} %fusion), channel_id=1, source_target_pairs={{0,2},{1,9},{8,10},{3,11},{16,18},{5,13},{24,26},{7,15},{32,34},{3... | collective-permute-start | bytes 589832 | tf_op jit(solution)/shard_map/ppermute | solution.py:28
  33.2 8.4 %collective-permute-start.9 = (f32[128,128]{1,0:T(8,128)S(1)}, f32[128,128]{1,0:T(8,128)S(1)}, u32[]{:S(2)}, u32[]{:S(2)}) collective-permute-start(f32[128,128]{1,0:T(8,128)S(1)} %broadcast_select_fusion.7.own), channel_id=1, source_target_pairs={{0,32},{1,33},{2,34},{3,35},{4,36},{5,37},{6,38},{7,39},{8,40},{9,... | collective-permute-start | bytes 196616 | tf_op jit(solution)/shard_map/ppermute | solution.py:28
  36.6 12.9 %collective-permute-start.7 = (f32[3,128,128]{2,1,0:T(8,128)S(1)}, f32[3,128,128]{2,1,0:T(8,128)S(1)}, u32[]{:S(2)}, u32[]{:S(2)}) collective-permute-start(f32[3,128,128]{2,1,0:T(8,128)S(1)} %broadcast_select_fusion), channel_id=1, source_target_pairs={{0,64},{1,65},{2,66},{3,67},{4,68},{5,69},{6,70},{7,71},{8,72},{9,... | collective-permute-start | bytes 589832 | tf_op jit(solution)/shard_map/ppermute | solution.py:28
  41.6 7.9 %collective-permute-start.10 = (f32[128,128]{1,0:T(8,128)S(1)}, f32[128,128]{1,0:T(8,128)S(1)}, u32[]{:S(2)}, u32[]{:S(2)}) collective-permute-start(f32[128,128]{1,0:T(8,128)S(1)} %broadcast_select_fusion.7.own), channel_id=1, source_target_pairs={{0,33},{1,32},{2,35},{3,34},{4,37},{5,36},{6,39},{7,38},{8,41},{9,... | collective-permute-start | bytes 196616 | tf_op jit(solution)/shard_map/ppermute | solution.py:28
  44.1 5.5 %collective-permute-start.8 = (f32[128,128]{1,0:T(8,128)S(1)}, f32[128,128]{1,0:T(8,128)S(1)}, u32[]{:S(2)}, u32[]{:S(2)}) collective-permute-start(f32[128,128]{1,0:T(8,128)S(1)} %broadcast_select_fusion.7.own), channel_id=1, source_target_pairs={{0,1},{1,0},{2,3},{3,2},{4,5},{5,4},{6,7},{7,6},{8,9},{9,8},{10,11... | collective-permute-start | bytes 196616 | tf_op jit(solution)/shard_map/ppermute | solution.py:28
  44.1 10.8 %collective-permute-start.20 = (f32[3,128,128]{2,1,0:T(8,128)S(1)}, f32[3,128,128]{2,1,0:T(8,128)S(1)}, u32[]{:S(2)}, u32[]{:S(2)}) collective-permute-start(f32[3,128,128]{2,1,0:T(8,128)S(1)} %select_select_fusion), channel_id=1, source_target_pairs={{0,24},{1,7},{2,26},{9,15},{4,28},{17,23},{6,30},{25,31},{8,0},{3,... | collective-permute-start | bytes 589832 | tf_op jit(solution)/shard_map/ppermute | solution.py:28
  44.2 10.7 %collective-permute-start.19 = (f32[3,128,128]{2,1,0:T(8,128)S(1)}, f32[3,128,128]{2,1,0:T(8,128)S(1)}, u32[]{:S(2)}, u32[]{:S(2)}) collective-permute-start(f32[3,128,128]{2,1,0:T(8,128)S(1)} %select_select_fusion), channel_id=1, source_target_pairs={{0,16},{1,5},{2,18},{9,13},{4,20},{17,21},{6,22},{25,29},{8,24},{3... | collective-permute-start | bytes 589832 | tf_op jit(solution)/shard_map/ppermute | solution.py:28
  49.5 5.7 %collective-permute-start.18 = (f32[3,128,128]{2,1,0:T(8,128)S(1)}, f32[3,128,128]{2,1,0:T(8,128)S(1)}, u32[]{:S(2)}, u32[]{:S(2)}) collective-permute-start(f32[3,128,128]{2,1,0:T(8,128)S(1)} %select_select_fusion), channel_id=1, source_target_pairs={{0,8},{1,3},{2,10},{9,11},{4,12},{17,19},{6,14},{25,27},{8,16},{3,... | collective-permute-start | bytes 589832 | tf_op jit(solution)/shard_map/ppermute | solution.py:28
  55.3 7.7 %collective-permute-start.21 = (f32[4,3,128,128]{3,2,1,0:T(8,128)S(1)}, f32[4,3,128,128]{3,2,1,0:T(8,128)S(1)}, u32[]{:S(2)}, u32[]{:S(2)}) collective-permute-start(f32[4,3,128,128]{3,2,1,0:T(8,128)S(1)} %pad_maximum_fusion.near), channel_id=1, source_target_pairs={{0,1},{1,0},{2,3},{3,2},{4,5},{5,4},{6,7},{7,6},{8,9},{9,8},{10,11... | collective-permute-start | bytes 2359304 | tf_op jit(solution)/shard_map/ppermute | solution.py:28
  55.4 7.6 %collective-permute-start.11 = (f32[3,128,128]{2,1,0:T(8,128)S(1)}, f32[3,128,128]{2,1,0:T(8,128)S(1)}, u32[]{:S(2)}, u32[]{:S(2)}) collective-permute-start(f32[3,128,128]{2,1,0:T(8,128)S(1)} %broadcast_select_fusion.1.part), channel_id=1, source_target_pairs={{0,32},{1,33},{2,34},{3,35},{4,36},{5,37},{6,38},{7,39},{8,40},{9,... | collective-permute-start | bytes 589832 | tf_op jit(solution)/shard_map/ppermute | solution.py:28

commit v3 on v2

--- a/solution.py
+++ b/solution.py
@@ -13,6 +13,7 @@
 ROW_TILES = 12
 COL_TILES = 3
 QUARTER = 3
+COLS = 32
 HIGHEST = lax.Precision.HIGHEST
 
 
@@ -91,26 +92,22 @@
     return lax.dot_general(a, b, dims, precision=HIGHEST, preferred_element_type=jnp.float32)
 
 
-def first_block(place, own, by_core, by_row, by_both, inv00, mixed, schur):
+def first_block(place, own, by_row, by_core, inv00, below, schur):
     odd_row = lax.rem(place[0], 2) == 1
     odd_col = lax.rem(place[1], 2) == 1
-    near_row = jnp.where(odd_col, by_core[...], own[...])
-    far_row = jnp.where(odd_col, by_both[...], by_row[...])
-    near_row_other = jnp.where(odd_col, own[...], by_core[...])
-    far_row_other = jnp.where(odd_col, by_row[...], by_both[...])
-    a00 = jnp.where(odd_row, far_row, near_row)
-    a10 = jnp.where(odd_row, near_row, far_row)
-    a11 = jnp.where(odd_row, near_row_other, far_row_other)
-    inv = inverse_factor(a00)
-    l10 = exact(a10, inv, transposed=True)
-    schur[...] = a11 - exact(l10, l10, transposed=True)
-    mixed[...] = exact(l10, inv)
+    upper = jnp.where(odd_row, by_row[...], own[...])
+    lower = jnp.where(odd_row, own[...], by_row[...])
+    inv = inverse_factor(jnp.where(odd_col, by_core[...], upper))
+    l10 = exact(jnp.where(odd_col, upper.T, lower), inv, transposed=True)
+    schur[...] = jnp.where(odd_col, lower, by_core[...]) - exact(l10, l10, transposed=True)
+    below[...] = l10
     inv00[...] = inv
 
 
-def second_block(inv00, mixed, schur, high, low):
+def second_block(inv00, below, schur, high, low):
+    mixed = exact(below[...], inv00[...])
     inv11 = inverse_factor(schur[...])
-    inv10 = -exact(inv11, mixed[...])
+    inv10 = -exact(inv11, mixed)
     zero = jnp.zeros((TB, TB), jnp.float32)
     for i, line in enumerate(((inv00[...], zero), (inv10, inv11))):
         for j, value in enumerate(line):
@@ -150,31 +147,15 @@
             s = quarter * QUARTER + i
             rows = slice(i * TB, (i + 1) * TB)
             for t in range(COL_TILES):
-                block[s, t] = block[s, t] - change[rows, t * TB : (t + 1) * TB]
-
-            @pl.when(my_col == 0)
-            def _():
-                block[s, 0] = left[rows, :TB]
-
-            @pl.when(my_col == 1)
-            def _():
-                block[s, 0] = left[rows, TB:]
-
-            if s == 0:
-
-                @pl.when(my_row < 2)
-                def _():
-                    for t in range(1, COL_TILES):
-                        block[0, t] = jnp.zeros((TB, TB), jnp.float32)
-
-                    @pl.when((my_col > 1) | (my_row < my_col))
-                    def _():
-                        block[0, 0] = jnp.zeros((TB, TB), jnp.float32)
-
-                    @pl.when(my_row == my_col)
-                    def _():
-                        block[0, 0] = jnp.where(lane <= sub, block[0, 0], 0.0)
-
+                value = block[s, t] - change[rows, t * TB : (t + 1) * TB]
+                if t == 0:
+                    panel = jnp.where(my_col == 0, left[rows, :TB], left[rows, TB:])
+                    value = jnp.where(my_col < 2, panel, value)
+                if s == 0:
+                    tile_col = t * COLS + my_col
+                    value = jnp.where((my_row < 2) & (tile_col > my_row), 0.0, value)
+                    value = jnp.where((my_row < 2) & (tile_col == my_row) & (lane > sub), 0.0, value)
+                block[s, t] = value
             pltpu.make_async_copy(block.at[s], out.at[s], sems.at[s]).start()
     for s in range(ROW_TILES):
         pltpu.make_async_copy(block.at[s], out.at[s], sems.at[s]).wait()
@@ -213,7 +194,6 @@
     my_v = jnp.where(my_core == 0, my_y, my_x)
     swap_core = [(device_of(z, c), device_of(z, c ^ 1)) for z in zs for c in cols]
     swap_row = [(device_of(z, c), device_of(z ^ 1, c)) for z in zs for c in cols]
-    swap_both = [(device_of(z, c), device_of(z ^ 1, c ^ 1)) for z in zs for c in cols]
     low_planes = (0, 1)
 
     column = tiles[:, 0].reshape(SIDE, QUARTER, TB, TB)
@@ -236,12 +216,10 @@
     got = send(diag3, plane_pairs(low_planes, sides, (0, 2), 0, 1))
     quarter1, quarter2, quarter3 = (after(q, diag3) for q in (quarter1, quarter2, quarter3))
     piece = jnp.where(my_u == 0, column[0], jnp.where(my_u == 1, quarter1, jnp.where(my_u == 2, quarter2, quarter3)))
-    piece1 = send(piece, plane_pairs(zs, sides, (0,), 0, 1))
+    far_piece = send(piece, plane_pairs(zs, sides, (0,), 0, 2))
     diag4 = jnp.where(my_v % 2 == 1, got, diag3)
 
     got = send(diag4, z_pairs(low_planes, 4, cols))
-    piece3 = send(after(piece, diag4), plane_pairs(zs, sides, (0,), 0, 3))
-    piece2 = send(after(piece, diag4), plane_pairs(zs, sides, (0,), 0, 2))
     diag5 = jnp.where((my_row == 4) | (my_row == 5), got, diag4)
 
     got = send(diag5, z_pairs((0, 1, 4, 5), 2, cols))
@@ -249,9 +227,11 @@
     part_got = send(part, z_pairs((0, 1, 4, 5), 2, cols))
     diag6 = jnp.where(my_row % 4 >= 2, got, diag5)
 
-    by_core, by_row, by_both = send(diag6, swap_core), send(diag6, swap_row), send(diag6, swap_both)
-    piece1, piece2, piece3 = (after(q, by_row) for q in (piece1, piece2, piece3))
-    piece = jnp.where(my_v == 0, piece, jnp.where(my_v == 1, piece1, jnp.where(my_v == 2, piece2, piece3)))
+    by_row = send(diag6, swap_row)
+    by_core = send(jnp.where(my_row % 2 == my_core, diag6, by_row), swap_core)
+    piece = jnp.where(my_v == 2, after(far_piece, diag5), piece)
+    piece1 = send(piece, plane_pairs(zs, sides, (0, 2), 0, 1))
+    piece = jnp.where(my_v % 2 == 1, after(piece1, by_row), piece)
     across = send(piece, plane_pairs(zs, sides, sides, 2, 0))
     up = send(piece, plane_pairs(zs, sides, sides, 1, 0))
     down = send(piece, plane_pairs(zs, sides, sides, 3, 0))
@@ -265,14 +245,14 @@
     anywhere = pl.BlockSpec(memory_space=pl.ANY)
     tile = jax.ShapeDtypeStruct((TB, TB), jnp.float32)
     inverse = jax.ShapeDtypeStruct((2 * TB, 2 * TB), jnp.bfloat16)
-    inv00, mixed, schur = pl.pallas_call(
+    inv00, below, schur = pl.pallas_call(
         first_block,
         out_shape=[tile] * 3,
-        in_specs=[smem] + [vmem] * 4,
+        in_specs=[smem] + [vmem] * 3,
         out_specs=[vmem] * 3,
         compiler_params=pltpu.CompilerParams(vmem_limit_bytes=8 * 1024 * 1024),
         name="first_block",
-    )(place, diag6, by_core, by_row, by_both)
+    )(place, diag6, by_row, by_core)
 
     up, down, across = (after(q, schur) for q in (up, down, across))
     near = jnp.stack([piece, up, across, down])
@@ -284,7 +264,7 @@
         out_specs=[vmem] * 2,
         compiler_params=pltpu.CompilerParams(vmem_limit_bytes=8 * 1024 * 1024),
         name="second_block",
-    )(inv00, mixed, schur)
+    )(inv00, below, schur)
 
     far, other_part = (after(q, high) for q in (far, other_part))
     result = pl.pallas_call(

time: 69.7 us -> 66.6 us (0.956)
  the two profiles are of different devices: /device:TPU:1 before, /device:TPU:200 now
where the time goes in v3:
time: 66.6 us; the launch traced here: 66.2 us
  waiting for transfers between devices  28.7 us (43%)
  starting transfers between devices  19.6 us (29%)
  Pallas kernels  13.9 us (21%)
  local copies, waits for them, and re-layouts  3.1 us (5%)
    ppermute x20, waiting for transfers between devices, send(): return lax.ppermute(value, ('row', 'col'), pairs)  28.7 us
    ppermute x20, starting transfers between devices, send(): return lax.ppermute(value, ('row', 'col'), pairs)  19.6 us
    pallas_call x1, Pallas kernels, shards(): pl.pallas_call(first_block, out_shape=[tile] * 3, in_specs=[smem] + [vmem...  5.29 us
    pallas_call x1, Pallas kernels, shards(): pl.pallas_call(update, out_shape=jax.ShapeDtypeStruct(tiles.shape, tiles....  4.42 us
    pallas_call x1, Pallas kernels, shards(): pl.pallas_call(second_block, out_shape=[inverse] * 2, in_specs=[vmem] * 3...  4.22 us
  transfers between devices with their start and end apart: 20, of which 5 were waited for; matrix products, arithmetic and copies ran while one was open for 4% of the time, Pallas kernels for 14%

profile of v3, /device:TPU:200, one launch (start us, length us, event | category | flops | bytes accessed | tf_op | source)
XLA Modules:
  0.0 66.2 jit_solution(1367949609479921800)
XLA Ops:
  0.0 1.0 %slice_bitcast_fusion.5 = f32[128,128]{1,0:T(8,128)S(1)} fusion(f32[12,3,128,128]{3,2,1,0:T(8,128)} %bitcast.28), kind=kLoop, calls=%fused_computation.11 | loop fusion | bytes 131072 | tf_op jit(solution)/shard_map/squeeze | solution.py:201
  1.0 0.7 collective-permute-start
  1.7 0.7 %collective-permute-start.1 = (f32[128,128]{1,0:T(8,128)S(1)}, f32[128,128]{1,0:T(8,128)S(1)}, u32[]{:S(2)}, u32[]{:S(2)}) collective-permute-start(f32[128,128]{1,0:T(8,128)S(1)} %broadcast_select_fusion.5), channel_id=1, source_target_pairs={{0,8},{1,3},{16,24},{5,7},{32,40},{33,35},{48,56},{37,39}} | collective-permute-start | bytes 196616 | tf_op jit(solution)/shard_map/ppermute | solution.py:29
  2.4 1.2 %slice_bitcast_fusion = (f32[3,128,128]{2,1,0:T(8,128)S(1)}, f32[3,128,128]{2,1,0:T(8,128)S(1)}, f32[3,128,128]{2,1,0:T(8,128)S(1)}) fusion(f32[12,3,128,128]{3,2,1,0:T(8,128)} %bitcast.29), kind=kLoop, calls=%fused_computation.1 | loop fusion | bytes 1179648 | tf_op jit(solution)/shard_map/squeeze | solution.py:204
  3.6 0.7 %collective-permute-start.13 = (f32[3,128,128]{2,1,0:T(8,128)S(1)}, f32[3,128,128]{2,1,0:T(8,128)S(1)}, u32[]{:S(2)}, u32[]{:S(2)}) collective-permute-start(f32[3,128,128]{2,1,0:T(8,128)S(1)} %get-tuple-element.43), channel_id=1, source_target_pairs={{0,24},{1,7},{32,56},{33,39},{64,88},{65,71},{96,120},{97,103},{12... | collective-permute-start | bytes 589832 | tf_op jit(solution)/shard_map/ppermute | solution.py:29
  4.3 1.3 %collective-permute-start.11 = (f32[3,128,128]{2,1,0:T(8,128)S(1)}, f32[3,128,128]{2,1,0:T(8,128)}, u32[]{:S(2)}, u32[]{:S(2)}) collective-permute-start(f32[3,128,128]{2,1,0:T(8,128)S(1)} %get-tuple-element.44), channel_id=1, source_target_pairs={{0,8},{1,3},{32,40},{33,35},{64,72},{65,67},{96,104},{97,99},{128,... | collective-permute-start | bytes 589832 | tf_op jit(solution)/shard_map/ppermute | solution.py:29
  5.6 0.7 %collective-permute-start.2 = (f32[128,128]{1,0:T(8,128)S(1)}, f32[128,128]{1,0:T(8,128)S(1)}, u32[]{:S(2)}, u32[]{:S(2)}) collective-permute-start(f32[128,128]{1,0:T(8,128)S(1)} %broadcast_select_fusion.6), channel_id=1, source_target_pairs={{0,4},{1,17},{8,12},{3,19},{16,20},{5,21},{24,28},{7,23},{32,36},{... | collective-permute-start | bytes 196616 | tf_op jit(solution)/shard_map/ppermute | solution.py:29
  6.3 0.9 %slice_bitcast_fusion.4 = f32[3,128,128]{2,1,0:T(8,128)S(1)} fusion(f32[12,3,128,128]{3,2,1,0:T(8,128)} %bitcast.30), kind=kLoop, calls=%fused_computation.6 | loop fusion | bytes 393216 | tf_op jit(solution)/shard_map/squeeze | solution.py:200
  7.3 0.7 %collective-permute-start.3 = (f32[128,128]{1,0:T(8,128)S(1)}, f32[128,128]{1,0:T(8,128)S(1)}, u32[]{:S(2)}, u32[]{:S(2)}) collective-permute-start(f32[128,128]{1,0:T(8,128)S(1)} %broadcast_select_fusion.7), channel_id=1, source_target_pairs={{0,2},{1,9},{4,6},{17,25},{8,10},{3,11},{12,14},{19,27},{16,18},{5... | collective-permute-start | bytes 196616 | tf_op jit(solution)/shard_map/ppermute | solution.py:29
  8.0 0.1 pad_add_fusion.place
  8.1 0.7 collective-permute-start.6
  8.7 0.7 %collective-permute-start.12 = (f32[3,128,128]{2,1,0:T(8,128)S(1)}, f32[3,128,128]{2,1,0:T(8,128)S(1)}, u32[]{:S(2)}, u32[]{:S(2)}) collective-permute-start(f32[3,128,128]{2,1,0:T(8,128)S(1)} %get-tuple-element.34), channel_id=1, source_target_pairs={{0,16},{1,5},{32,48},{33,37},{64,80},{65,69},{96,112},{97,101},{12... | collective-permute-start | bytes 589832 | tf_op jit(solution)/shard_map/ppermute | solution.py:29
  9.5 0.7 %collective-permute-start.4 = (f32[128,128]{1,0:T(8,128)S(1)}, f32[128,128]{1,0:T(8,128)S(1)}, u32[]{:S(2)}, u32[]{:S(2)}) collective-permute-start(f32[128,128]{1,0:T(8,128)S(1)} %broadcast_select_fusion.8), channel_id=1, source_target_pairs={{0,128},{1,129},{2,130},{3,131},{4,132},{5,133},{6,134},{7,135},{8... | collective-permute-start | bytes 196616 | tf_op jit(solution)/shard_map/ppermute | solution.py:29
  10.2 0.7 %collective-permute-start.14 = (f32[3,128,128]{2,1,0:T(8,128)S(1)}, f32[3,128,128]{2,1,0:T(8,128)S(1)}, u32[]{:S(2)}, u32[]{:S(2)}) collective-permute-start(f32[3,128,128]{2,1,0:T(8,128)S(1)} %fusion), channel_id=1, source_target_pairs={{0,4},{1,17},{8,12},{3,19},{16,20},{5,21},{24,28},{7,23},{32,36},{... | collective-permute-start | bytes 589832 | tf_op jit(solution)/shard_map/ppermute | solution.py:29
  10.9 1.3 %collective-permute-start.5 = (f32[128,128]{1,0:T(8,128)S(1)}, f32[128,128]{1,0:T(8,128)S(1)}, u32[]{:S(2)}, u32[]{:S(2)}) collective-permute-start(f32[128,128]{1,0:T(8,128)S(1)} %broadcast_select_fusion.9), channel_id=1, source_target_pairs={{0,64},{1,65},{2,66},{3,67},{4,68},{5,69},{6,70},{7,71},{8,72},{9,... | collective-permute-start | bytes 196616 | tf_op jit(solution)/shard_map/ppermute | solution.py:29
  12.3 1.3 %collective-permute-start.7 = (f32[3,128,128]{2,1,0:T(8,128)S(1)}, f32[3,128,128]{2,1,0:T(8,128)S(1)}, u32[]{:S(2)}, u32[]{:S(2)}) collective-permute-start(f32[3,128,128]{2,1,0:T(8,128)S(1)} %broadcast_select_fusion.2), channel_id=1, source_target_pairs={{0,64},{1,65},{2,66},{3,67},{4,68},{5,69},{6,70},{7,71},{8,72},{9,... | collective-permute-start | bytes 589832 | tf_op jit(solution)/shard_map/ppermute | solution.py:29
  13.6 15.2 %collective-permute-done.5 = f32[128,128]{1,0:T(8,128)S(1)} collective-permute-done((f32[128,128]{1,0:T(8,128)S(1)}, f32[128,128]{1,0:T(8,128)S(1)}, u32[]{:S(2)}, u32[]{:S(2)}) %collective-permute-start.5) | collective-permute-done | bytes 65568 | tf_op jit(solution)/shard_map/ppermute | solution.py:29
  28.8 5.8 %collective-permute-start.8 = (f32[128,128]{1,0:T(8,128)S(1)}, f32[128,128]{1,0:T(8,128)S(1)}, u32[]{:S(2)}, u32[]{:S(2)}) collective-permute-start(f32[128,128]{1,0:T(8,128)S(1)} %broadcast_select_fusion.10.own), channel_id=1, source_target_pairs={{0,32},{1,33},{2,34},{3,35},{4,36},{5,37},{6,38},{7,39},{8,40},{9,... | collective-permute-start | bytes 196616 | tf_op jit(solution)/shard_map/ppermute | solution.py:29
  34.6 1.3 %collective-permute-start.15 = (f32[3,128,128]{2,1,0:T(8,128)S(1)}, f32[3,128,128]{2,1,0:T(8,128)S(1)}, u32[]{:S(2)}, u32[]{:S(2)}) collective-permute-start(f32[3,128,128]{2,1,0:T(8,128)S(1)} %broadcast_select_fusion), channel_id=1, source_target_pairs={{0,2},{1,9},{4,6},{17,25},{8,10},{3,11},{12,14},{19,27},{16,18},{5... | collective-permute-start | bytes 589832 | tf_op jit(solution)/shard_map/ppermute | solution.py:29
  35.9 0.9 %collective-permute-done.8.by_row = f32[128,128]{1,0:T(8,128)S(1)} collective-permute-done((f32[128,128]{1,0:T(8,128)S(1)}, f32[128,128]{1,0:T(8,128)S(1)}, u32[]{:S(2)}, u32[]{:S(2)}) %collective-permute-start.8) | collective-permute-done | bytes 65568 | tf_op jit(solution)/shard_map/ppermute | solution.py:29
  36.9 0.1 collective-permute-start.9
  37.0 7.7 %collective-permute-done.15 = f32[3,128,128]{2,1,0:T(8,128)S(1)} collective-permute-done((f32[3,128,128]{2,1,0:T(8,128)S(1)}, f32[3,128,128]{2,1,0:T(8,128)S(1)}, u32[]{:S(2)}, u32[]{:S(2)}) %collective-permute-start.15) | collective-permute-done | bytes 196640 | tf_op jit(solution)/shard_map/ppermute | solution.py:29
  44.7 0.1 collective-permute-start.18
  44.8 0.4 collective-permute-start.17
  45.2 1.7 %collective-permute-start.16 = (f32[3,128,128]{2,1,0:T(8,128)S(1)}, f32[3,128,128]{2,1,0:T(8,128)S(1)}, u32[]{:S(2)}, u32[]{:S(2)}) collective-permute-start(f32[3,128,128]{2,1,0:T(8,128)S(1)} %broadcast_select_fusion.1), channel_id=1, source_target_pairs={{0,8},{1,3},{2,10},{9,11},{4,12},{17,19},{6,14},{25,27},{8,16},{3,... | collective-permute-start | bytes 589832 | tf_op jit(solution)/shard_map/ppermute | solution.py:29
  46.9 5.3 %first_block.1 = (f32[128,128]{1,0:T(8,128)S(1)}, f32[128,128]{1,0:T(8,128)S(1)}, f32[128,128]{1,0:T(8,128)S(1)}) custom-call(s32[2]{0:T(128)S(1)} %pad_add_fusion.place, f32[128,128]{1,0:T(8,128)S(1)} %broadcast_select_fusion.10.own, f32[128,128]{1,0:T(8,128)S(1)} %collective-permute-done.8.by_row, f32[128,128]{1,0:T(8,128)S(1)} %collective-permute-done.9.by_core), custom_call_target="tpu_custom_call" | custom-call | tf_op jit(solution)/shard_map/first_block/pallas_call | solution.py:248
  52.2 2.0 %collective-permute-done.16 = f32[3,128,128]{2,1,0:T(8,128)S(1)} collective-permute-done((f32[3,128,128]{2,1,0:T(8,128)S(1)}, f32[3,128,128]{2,1,0:T(8,128)S(1)}, u32[]{:S(2)}, u32[]{:S(2)}) %collective-permute-start.16) | collective-permute-done | bytes 196640 | tf_op jit(solution)/shard_map/ppermute | solution.py:29
  54.2 0.1 collective-permute-start.19
  54.3 0.3 collective-permute-start.10
  54.6 4.2 %second_block.1 = (bf16[256,256]{1,0:T(8,128)(2,1)S(1)}, bf16[256,256]{1,0:T(8,128)(2,1)S(1)}) custom-call(f32[128,128]{1,0:T(8,128)S(1)} %get-tuple-element.27.inv00, f32[128,128]{1,0:T(8,128)S(1)} %get-tuple-element.28.below, f32[128,128]{1,0:T(8,128)S(1)} %get-tuple-element.29.schur), custom_call_target="tpu_custom_call" | custom-call | tf_op jit(solution)/shard_map/second_block/pallas_call | solution.py:260
  58.8 2.8 %collective-permute-done.10.other_part = f32[3,128,128]{2,1,0:T(8,128)S(1)} collective-permute-done((f32[3,128,128]{2,1,0:T(8,128)S(1)}, f32[3,128,128]{2,1,0:T(8,128)S(1)}, u32[]{:S(2)}, u32[]{:S(2)}) %collective-permute-start.10) | collective-permute-done | bytes 196640 | tf_op jit(solution)/shard_map/ppermute | solution.py:29
  61.6 4.4 %update.1 = f32[12,3,128,128]{3,2,1,0:T(8,128)} custom-call(s32[2]{0:T(128)S(1)} %pad_add_fusion.place, bf16[256,256]{1,0:T(8,128)(2,1)S(1)} %get-tuple-element.30.high, bf16[256,256]{1,0:T(8,128)(2,1)S(1)} %get-tuple-element.31.low, f32[3,128,128]{2,1,0:T(8,128)S(1)} %broadcast_select_fusion.3.part, f32[3,128,128]{2,1,0:T(8,128)S(1)} %collective-permute-done.10.other_part, ...), custom_call_target="tpu_custom_call" | custom-call | tf_op jit(solution)/shard_map/update/pallas_call | solution.py:270
  (30 shorter events, 0.3 us)
Async XLA Ops:
  0.0 10.2 %copy-start = (f32[12,128,3,128]{3,1,2,0:T(8,128)S(1)}, f32[12,128,3,128]{3,1,2,0:T(8,128)}, u32[]{:S(2)}) copy-start(f32[12,128,3,128]{3,1,2,0:T(8,128)} %param.1) | copy-start | bytes 7077892
  1.0 0.7 %collective-permute-start = (f32[128,128]{1,0:T(8,128)S(1)}, f32[128,128]{1,0:T(8,128)S(1)}, u32[]{:S(2)}, u32[]{:S(2)}) collective-permute-start(f32[128,128]{1,0:T(8,128)S(1)} %slice_bitcast_fusion.5), channel_id=1, source_target_pairs={{0,16},{1,5},{32,48},{33,37}} | collective-permute-start | bytes 196616 | tf_op jit(solution)/shard_map/ppermute | solution.py:29
  1.7 3.9 %collective-permute-start.1 = (f32[128,128]{1,0:T(8,128)S(1)}, f32[128,128]{1,0:T(8,128)S(1)}, u32[]{:S(2)}, u32[]{:S(2)}) collective-permute-start(f32[128,128]{1,0:T(8,128)S(1)} %broadcast_select_fusion.5), channel_id=1, source_target_pairs={{0,8},{1,3},{16,24},{5,7},{32,40},{33,35},{48,56},{37,39}} | collective-permute-start | bytes 196616 | tf_op jit(solution)/shard_map/ppermute | solution.py:29
  3.6 5.8 %collective-permute-start.13 = (f32[3,128,128]{2,1,0:T(8,128)S(1)}, f32[3,128,128]{2,1,0:T(8,128)S(1)}, u32[]{:S(2)}, u32[]{:S(2)}) collective-permute-start(f32[3,128,128]{2,1,0:T(8,128)S(1)} %get-tuple-element.43), channel_id=1, source_target_pairs={{0,24},{1,7},{32,56},{33,39},{64,88},{65,71},{96,120},{97,103},{12... | collective-permute-start | bytes 589832 | tf_op jit(solution)/shard_map/ppermute | solution.py:29
  4.3 5.2 %collective-permute-start.11 = (f32[3,128,128]{2,1,0:T(8,128)S(1)}, f32[3,128,128]{2,1,0:T(8,128)}, u32[]{:S(2)}, u32[]{:S(2)}) collective-permute-start(f32[3,128,128]{2,1,0:T(8,128)S(1)} %get-tuple-element.44), channel_id=1, source_target_pairs={{0,8},{1,3},{32,40},{33,35},{64,72},{65,67},{96,104},{97,99},{128,... | collective-permute-start | bytes 589832 | tf_op jit(solution)/shard_map/ppermute | solution.py:29
  5.6 1.7 %collective-permute-start.2 = (f32[128,128]{1,0:T(8,128)S(1)}, f32[128,128]{1,0:T(8,128)S(1)}, u32[]{:S(2)}, u32[]{:S(2)}) collective-permute-start(f32[128,128]{1,0:T(8,128)S(1)} %broadcast_select_fusion.6), channel_id=1, source_target_pairs={{0,4},{1,17},{8,12},{3,19},{16,20},{5,21},{24,28},{7,23},{32,36},{... | collective-permute-start | bytes 196616 | tf_op jit(solution)/shard_map/ppermute | solution.py:29
  7.3 2.1 %collective-permute-start.3 = (f32[128,128]{1,0:T(8,128)S(1)}, f32[128,128]{1,0:T(8,128)S(1)}, u32[]{:S(2)}, u32[]{:S(2)}) collective-permute-start(f32[128,128]{1,0:T(8,128)S(1)} %broadcast_select_fusion.7), channel_id=1, source_target_pairs={{0,2},{1,9},{4,6},{17,25},{8,10},{3,11},{12,14},{19,27},{16,18},{5... | collective-permute-start | bytes 196616 | tf_op jit(solution)/shard_map/ppermute | solution.py:29
  8.1 4.2 %collective-permute-start.6 = (f32[3,128,128]{2,1,0:T(8,128)S(1)}, f32[3,128,128]{2,1,0:T(8,128)S(1)}, u32[]{:S(2)}, u32[]{:S(2)}) collective-permute-start(f32[3,128,128]{2,1,0:T(8,128)S(1)} %slice_bitcast_fusion.4), channel_id=1, source_target_pairs={{0,128},{1,129},{2,130},{3,131},{4,132},{5,133},{6,134},{7,135},{8... | collective-permute-start | bytes 589832 | tf_op jit(solution)/shard_map/ppermute | solution.py:29
  8.7 1.4 %collective-permute-start.12 = (f32[3,128,128]{2,1,0:T(8,128)S(1)}, f32[3,128,128]{2,1,0:T(8,128)S(1)}, u32[]{:S(2)}, u32[]{:S(2)}) collective-permute-start(f32[3,128,128]{2,1,0:T(8,128)S(1)} %get-tuple-element.34), channel_id=1, source_target_pairs={{0,16},{1,5},{32,48},{33,37},{64,80},{65,69},{96,112},{97,101},{12... | collective-permute-start | bytes 589832 | tf_op jit(solution)/shard_map/ppermute | solution.py:29
  9.5 1.4 %collective-permute-start.4 = (f32[128,128]{1,0:T(8,128)S(1)}, f32[128,128]{1,0:T(8,128)S(1)}, u32[]{:S(2)}, u32[]{:S(2)}) collective-permute-start(f32[128,128]{1,0:T(8,128)S(1)} %broadcast_select_fusion.8), channel_id=1, source_target_pairs={{0,128},{1,129},{2,130},{3,131},{4,132},{5,133},{6,134},{7,135},{8... | collective-permute-start | bytes 196616 | tf_op jit(solution)/shard_map/ppermute | solution.py:29
  10.2 24.4 %collective-permute-start.14 = (f32[3,128,128]{2,1,0:T(8,128)S(1)}, f32[3,128,128]{2,1,0:T(8,128)S(1)}, u32[]{:S(2)}, u32[]{:S(2)}) collective-permute-start(f32[3,128,128]{2,1,0:T(8,128)S(1)} %fusion), channel_id=1, source_target_pairs={{0,4},{1,17},{8,12},{3,19},{16,20},{5,21},{24,28},{7,23},{32,36},{... | collective-permute-start | bytes 589832 | tf_op jit(solution)/shard_map/ppermute | solution.py:29
  10.9 17.8 %collective-permute-start.5 = (f32[128,128]{1,0:T(8,128)S(1)}, f32[128,128]{1,0:T(8,128)S(1)}, u32[]{:S(2)}, u32[]{:S(2)}) collective-permute-start(f32[128,128]{1,0:T(8,128)S(1)} %broadcast_select_fusion.9), channel_id=1, source_target_pairs={{0,64},{1,65},{2,66},{3,67},{4,68},{5,69},{6,70},{7,71},{8,72},{9,... | collective-permute-start | bytes 196616 | tf_op jit(solution)/shard_map/ppermute | solution.py:29
  12.3 34.5 %collective-permute-start.7 = (f32[3,128,128]{2,1,0:T(8,128)S(1)}, f32[3,128,128]{2,1,0:T(8,128)S(1)}, u32[]{:S(2)}, u32[]{:S(2)}) collective-permute-start(f32[3,128,128]{2,1,0:T(8,128)S(1)} %broadcast_select_fusion.2), channel_id=1, source_target_pairs={{0,64},{1,65},{2,66},{3,67},{4,68},{5,69},{6,70},{7,71},{8,72},{9,... | collective-permute-start | bytes 589832 | tf_op jit(solution)/shard_map/ppermute | solution.py:29
  28.8 8.1 %collective-permute-start.8 = (f32[128,128]{1,0:T(8,128)S(1)}, f32[128,128]{1,0:T(8,128)S(1)}, u32[]{:S(2)}, u32[]{:S(2)}) collective-permute-start(f32[128,128]{1,0:T(8,128)S(1)} %broadcast_select_fusion.10.own), channel_id=1, source_target_pairs={{0,32},{1,33},{2,34},{3,35},{4,36},{5,37},{6,38},{7,39},{8,40},{9,... | collective-permute-start | bytes 196616 | tf_op jit(solution)/shard_map/ppermute | solution.py:29
  34.6 10.1 %collective-permute-start.15 = (f32[3,128,128]{2,1,0:T(8,128)S(1)}, f32[3,128,128]{2,1,0:T(8,128)S(1)}, u32[]{:S(2)}, u32[]{:S(2)}) collective-permute-start(f32[3,128,128]{2,1,0:T(8,128)S(1)} %broadcast_select_fusion), channel_id=1, source_target_pairs={{0,2},{1,9},{4,6},{17,25},{8,10},{3,11},{12,14},{19,27},{16,18},{5... | collective-permute-start | bytes 589832 | tf_op jit(solution)/shard_map/ppermute | solution.py:29
  36.9 10.0 %collective-permute-start.9 = (f32[128,128]{1,0:T(8,128)S(1)}, f32[128,128]{1,0:T(8,128)S(1)}, u32[]{:S(2)}, u32[]{:S(2)}) collective-permute-start(f32[128,128]{1,0:T(8,128)S(1)} %broadcast_select_fusion.4), channel_id=1, source_target_pairs={{0,1},{1,0},{2,3},{3,2},{4,5},{5,4},{6,7},{7,6},{8,9},{9,8},{10,11... | collective-permute-start | bytes 196616 | tf_op jit(solution)/shard_map/ppermute | solution.py:29
  44.7 7.4 %collective-permute-start.18 = (f32[3,128,128]{2,1,0:T(8,128)S(1)}, f32[3,128,128]{2,1,0:T(8,128)S(1)}, u32[]{:S(2)}, u32[]{:S(2)}) collective-permute-start(f32[3,128,128]{2,1,0:T(8,128)S(1)} %broadcast_select_fusion.1), channel_id=1, source_target_pairs={{0,24},{1,7},{2,26},{9,15},{4,28},{17,23},{6,30},{25,31},{8,0},{3,... | collective-permute-start | bytes 589832 | tf_op jit(solution)/shard_map/ppermute | solution.py:29
  44.8 7.4 %collective-permute-start.17 = (f32[3,128,128]{2,1,0:T(8,128)S(1)}, f32[3,128,128]{2,1,0:T(8,128)S(1)}, u32[]{:S(2)}, u32[]{:S(2)}) collective-permute-start(f32[3,128,128]{2,1,0:T(8,128)S(1)} %broadcast_select_fusion.1), channel_id=1, source_target_pairs={{0,16},{1,5},{2,18},{9,13},{4,20},{17,21},{6,22},{25,29},{8,24},{3... | collective-permute-start | bytes 589832 | tf_op jit(solution)/shard_map/ppermute | solution.py:29
  45.2 9.0 %collective-permute-start.16 = (f32[3,128,128]{2,1,0:T(8,128)S(1)}, f32[3,128,128]{2,1,0:T(8,128)S(1)}, u32[]{:S(2)}, u32[]{:S(2)}) collective-permute-start(f32[3,128,128]{2,1,0:T(8,128)S(1)} %broadcast_select_fusion.1), channel_id=1, source_target_pairs={{0,8},{1,3},{2,10},{9,11},{4,12},{17,19},{6,14},{25,27},{8,16},{3,... | collective-permute-start | bytes 589832 | tf_op jit(solution)/shard_map/ppermute | solution.py:29
  54.2 7.4 %collective-permute-start.19 = (f32[4,3,128,128]{3,2,1,0:T(8,128)S(1)}, f32[4,3,128,128]{3,2,1,0:T(8,128)S(1)}, u32[]{:S(2)}, u32[]{:S(2)}) collective-permute-start(f32[4,3,128,128]{3,2,1,0:T(8,128)S(1)} %pad_maximum_fusion.near), channel_id=1, source_target_pairs={{0,1},{1,0},{2,3},{3,2},{4,5},{5,4},{6,7},{7,6},{8,9},{9,8},{10,11... | collective-permute-start | bytes 2359304 | tf_op jit(solution)/shard_map/ppermute | solution.py:29
  54.3 7.3 %collective-permute-start.10 = (f32[3,128,128]{2,1,0:T(8,128)S(1)}, f32[3,128,128]{2,1,0:T(8,128)S(1)}, u32[]{:S(2)}, u32[]{:S(2)}) collective-permute-start(f32[3,128,128]{2,1,0:T(8,128)S(1)} %broadcast_select_fusion.3.part), channel_id=1, source_target_pairs={{0,32},{1,33},{2,34},{3,35},{4,36},{5,37},{6,38},{7,39},{8,40},{9,... | collective-permute-start | bytes 589832 | tf_op jit(solution)/shard_map/ppermute | solution.py:29

commit v4 on v3

--- a/solution.py
+++ b/solution.py
@@ -95,11 +95,11 @@
 def first_block(place, own, by_row, by_core, inv00, below, schur):
     odd_row = lax.rem(place[0], 2) == 1
     odd_col = lax.rem(place[1], 2) == 1
-    upper = jnp.where(odd_row, by_row[...], own[...])
-    lower = jnp.where(odd_row, own[...], by_row[...])
-    inv = inverse_factor(jnp.where(odd_col, by_core[...], upper))
-    l10 = exact(jnp.where(odd_col, upper.T, lower), inv, transposed=True)
-    schur[...] = jnp.where(odd_col, lower, by_core[...]) - exact(l10, l10, transposed=True)
+    left = jnp.where(odd_col, by_core[...], own[...])
+    right = jnp.where(odd_col, own[...], by_core[...])
+    inv = inverse_factor(jnp.where(odd_row, by_row[...], left))
+    l10 = exact(jnp.where(odd_row, left, right.T), inv, transposed=True)
+    schur[...] = jnp.where(odd_row, right, by_row[...]) - exact(l10, l10, transposed=True)
     below[...] = l10
     inv00[...] = inv
 
@@ -227,11 +227,11 @@
     part_got = send(part, z_pairs((0, 1, 4, 5), 2, cols))
     diag6 = jnp.where(my_row % 4 >= 2, got, diag5)
 
-    by_row = send(diag6, swap_row)
-    by_core = send(jnp.where(my_row % 2 == my_core, diag6, by_row), swap_core)
+    by_core = send(diag6, swap_core)
+    by_row = send(jnp.where(my_row % 2 == my_core, diag6, by_core), swap_row)
     piece = jnp.where(my_v == 2, after(far_piece, diag5), piece)
     piece1 = send(piece, plane_pairs(zs, sides, (0, 2), 0, 1))
-    piece = jnp.where(my_v % 2 == 1, after(piece1, by_row), piece)
+    piece = jnp.where(my_v % 2 == 1, after(piece1, diag6), piece)
     across = send(piece, plane_pairs(zs, sides, sides, 2, 0))
     up = send(piece, plane_pairs(zs, sides, sides, 1, 0))
     down = send(piece, plane_pairs(zs, sides, sides, 3, 0))

time: 66.6 us -> 65.2 us (0.979); the launches traced: 66.2 us -> 63.9 us
  waiting for transfers between devices: 28.7 us -> 20 us
  starting transfers between devices: 19.6 us -> 26 us
    ppermute x20, waiting for transfers between devices: 28.7 us -> 20 us  [send(): return lax.ppermute(value, ('row', 'col'), pairs)]
    ppermute x20, starting transfers between devices: 19.6 us -> 26 us  [send(): return lax.ppermute(value, ('row', 'col'), pairs)]
  transfers between devices with their start and end apart: 20 -> 20, of which waited for: 5 -> 4; matrix products, arithmetic and copies ran while one was open for 4% -> 4% of each run, Pallas kernels for 14% -> 15%
where the time goes in v4:
time: 65.2 us; the launch traced here: 63.9 us
  starting transfers between devices  26 us (40%)
  waiting for transfers between devices  20 us (31%)
  Pallas kernels  13.9 us (21%)
  local copies, waits for them, and re-layouts  3.1 us (5%)
    ppermute x20, starting transfers between devices, send(): return lax.ppermute(value, ('row', 'col'), pairs)  26 us
    ppermute x20, waiting for transfers between devices, send(): return lax.ppermute(value, ('row', 'col'), pairs)  20 us
    pallas_call x1, Pallas kernels, shards(): pl.pallas_call(first_block, out_shape=[tile] * 3, in_specs=[smem] + [vmem...  5.29 us
    pallas_call x1, Pallas kernels, shards(): pl.pallas_call(update, out_shape=jax.ShapeDtypeStruct(tiles.shape, tiles....  4.42 us
    pallas_call x1, Pallas kernels, shards(): pl.pallas_call(second_block, out_shape=[inverse] * 2, in_specs=[vmem] * 3...  4.22 us
  transfers between devices with their start and end apart: 20, of which 4 were waited for; matrix products, arithmetic and copies ran while one was open for 4% of the time, Pallas kernels for 15%

profile of v4, /device:TPU:200, one launch (start us, length us, event | category | flops | bytes accessed | tf_op | source)
XLA Modules:
  0.0 63.9 jit_solution(14865457161670324039)
XLA Ops:
  0.0 1.0 %slice_bitcast_fusion.5 = f32[128,128]{1,0:T(8,128)S(1)} fusion(f32[12,3,128,128]{3,2,1,0:T(8,128)} %bitcast.28), kind=kLoop, calls=%fused_computation.11 | loop fusion | bytes 131072 | tf_op jit(solution)/shard_map/squeeze | solution.py:201
  1.0 0.7 %collective-permute-start = (f32[128,128]{1,0:T(8,128)S(1)}, f32[128,128]{1,0:T(8,128)S(1)}, u32[]{:S(2)}, u32[]{:S(2)}) collective-permute-start(f32[128,128]{1,0:T(8,128)S(1)} %slice_bitcast_fusion.5), channel_id=1, source_target_pairs={{0,16},{1,5},{32,48},{33,37}} | collective-permute-start | bytes 196616 | tf_op jit(solution)/shard_map/ppermute | solution.py:29
  1.7 0.7 %collective-permute-start.1 = (f32[128,128]{1,0:T(8,128)S(1)}, f32[128,128]{1,0:T(8,128)S(1)}, u32[]{:S(2)}, u32[]{:S(2)}) collective-permute-start(f32[128,128]{1,0:T(8,128)S(1)} %broadcast_select_fusion.5), channel_id=1, source_target_pairs={{0,8},{1,3},{16,24},{5,7},{32,40},{33,35},{48,56},{37,39}} | collective-permute-start | bytes 196616 | tf_op jit(solution)/shard_map/ppermute | solution.py:29
  2.4 1.2 %slice_bitcast_fusion = (f32[3,128,128]{2,1,0:T(8,128)S(1)}, f32[3,128,128]{2,1,0:T(8,128)S(1)}, f32[3,128,128]{2,1,0:T(8,128)S(1)}) fusion(f32[12,3,128,128]{3,2,1,0:T(8,128)} %bitcast.29), kind=kLoop, calls=%fused_computation.1 | loop fusion | bytes 1179648 | tf_op jit(solution)/shard_map/squeeze | solution.py:204
  3.6 0.7 %collective-permute-start.13 = (f32[3,128,128]{2,1,0:T(8,128)S(1)}, f32[3,128,128]{2,1,0:T(8,128)S(1)}, u32[]{:S(2)}, u32[]{:S(2)}) collective-permute-start(f32[3,128,128]{2,1,0:T(8,128)S(1)} %get-tuple-element.43), channel_id=1, source_target_pairs={{0,24},{1,7},{32,56},{33,39},{64,88},{65,71},{96,120},{97,103},{12... | collective-permute-start | bytes 589832 | tf_op jit(solution)/shard_map/ppermute | solution.py:29
  4.3 1.3 %collective-permute-start.11 = (f32[3,128,128]{2,1,0:T(8,128)S(1)}, f32[3,128,128]{2,1,0:T(8,128)}, u32[]{:S(2)}, u32[]{:S(2)}) collective-permute-start(f32[3,128,128]{2,1,0:T(8,128)S(1)} %get-tuple-element.44), channel_id=1, source_target_pairs={{0,8},{1,3},{32,40},{33,35},{64,72},{65,67},{96,104},{97,99},{128,... | collective-permute-start | bytes 589832 | tf_op jit(solution)/shard_map/ppermute | solution.py:29
  5.6 0.7 %collective-permute-start.2 = (f32[128,128]{1,0:T(8,128)S(1)}, f32[128,128]{1,0:T(8,128)S(1)}, u32[]{:S(2)}, u32[]{:S(2)}) collective-permute-start(f32[128,128]{1,0:T(8,128)S(1)} %broadcast_select_fusion.6), channel_id=1, source_target_pairs={{0,4},{1,17},{8,12},{3,19},{16,20},{5,21},{24,28},{7,23},{32,36},{... | collective-permute-start | bytes 196616 | tf_op jit(solution)/shard_map/ppermute | solution.py:29
  6.3 0.9 %slice_bitcast_fusion.4 = f32[3,128,128]{2,1,0:T(8,128)S(1)} fusion(f32[12,3,128,128]{3,2,1,0:T(8,128)} %bitcast.30), kind=kLoop, calls=%fused_computation.6 | loop fusion | bytes 393216 | tf_op jit(solution)/shard_map/squeeze | solution.py:200
  7.3 0.7 %collective-permute-start.3 = (f32[128,128]{1,0:T(8,128)S(1)}, f32[128,128]{1,0:T(8,128)S(1)}, u32[]{:S(2)}, u32[]{:S(2)}) collective-permute-start(f32[128,128]{1,0:T(8,128)S(1)} %broadcast_select_fusion.7), channel_id=1, source_target_pairs={{0,2},{1,9},{4,6},{17,25},{8,10},{3,11},{12,14},{19,27},{16,18},{5... | collective-permute-start | bytes 196616 | tf_op jit(solution)/shard_map/ppermute | solution.py:29
  8.0 0.1 pad_add_fusion.place
  8.1 0.7 %collective-permute-start.6 = (f32[3,128,128]{2,1,0:T(8,128)S(1)}, f32[3,128,128]{2,1,0:T(8,128)S(1)}, u32[]{:S(2)}, u32[]{:S(2)}) collective-permute-start(f32[3,128,128]{2,1,0:T(8,128)S(1)} %slice_bitcast_fusion.4), channel_id=1, source_target_pairs={{0,128},{1,129},{2,130},{3,131},{4,132},{5,133},{6,134},{7,135},{8... | collective-permute-start | bytes 589832 | tf_op jit(solution)/shard_map/ppermute | solution.py:29
  8.7 0.7 %collective-permute-start.12 = (f32[3,128,128]{2,1,0:T(8,128)S(1)}, f32[3,128,128]{2,1,0:T(8,128)S(1)}, u32[]{:S(2)}, u32[]{:S(2)}) collective-permute-start(f32[3,128,128]{2,1,0:T(8,128)S(1)} %get-tuple-element.34), channel_id=1, source_target_pairs={{0,16},{1,5},{32,48},{33,37},{64,80},{65,69},{96,112},{97,101},{12... | collective-permute-start | bytes 589832 | tf_op jit(solution)/shard_map/ppermute | solution.py:29
  9.5 0.7 %collective-permute-start.4 = (f32[128,128]{1,0:T(8,128)S(1)}, f32[128,128]{1,0:T(8,128)S(1)}, u32[]{:S(2)}, u32[]{:S(2)}) collective-permute-start(f32[128,128]{1,0:T(8,128)S(1)} %broadcast_select_fusion.8), channel_id=1, source_target_pairs={{0,128},{1,129},{2,130},{3,131},{4,132},{5,133},{6,134},{7,135},{8... | collective-permute-start | bytes 196616 | tf_op jit(solution)/shard_map/ppermute | solution.py:29
  10.2 0.1 fusion
  10.2 0.7 %collective-permute-start.14 = (f32[3,128,128]{2,1,0:T(8,128)S(1)}, f32[3,128,128]{2,1,0:T(8,128)S(1)}, u32[]{:S(2)}, u32[]{:S(2)}) collective-permute-start(f32[3,128,128]{2,1,0:T(8,128)S(1)} %fusion), channel_id=1, source_target_pairs={{0,4},{1,17},{8,12},{3,19},{16,20},{5,21},{24,28},{7,23},{32,36},{... | collective-permute-start | bytes 589832 | tf_op jit(solution)/shard_map/ppermute | solution.py:29
  10.9 1.3 %collective-permute-start.5 = (f32[128,128]{1,0:T(8,128)S(1)}, f32[128,128]{1,0:T(8,128)S(1)}, u32[]{:S(2)}, u32[]{:S(2)}) collective-permute-start(f32[128,128]{1,0:T(8,128)S(1)} %broadcast_select_fusion.9), channel_id=1, source_target_pairs={{0,64},{1,65},{2,66},{3,67},{4,68},{5,69},{6,70},{7,71},{8,72},{9,... | collective-permute-start | bytes 196616 | tf_op jit(solution)/shard_map/ppermute | solution.py:29
  12.3 1.3 %collective-permute-start.7 = (f32[3,128,128]{2,1,0:T(8,128)S(1)}, f32[3,128,128]{2,1,0:T(8,128)S(1)}, u32[]{:S(2)}, u32[]{:S(2)}) collective-permute-start(f32[3,128,128]{2,1,0:T(8,128)S(1)} %broadcast_select_fusion.2), channel_id=1, source_target_pairs={{0,64},{1,65},{2,66},{3,67},{4,68},{5,69},{6,70},{7,71},{8,72},{9,... | collective-permute-start | bytes 589832 | tf_op jit(solution)/shard_map/ppermute | solution.py:29
  13.6 15.2 %collective-permute-done.5 = f32[128,128]{1,0:T(8,128)S(1)} collective-permute-done((f32[128,128]{1,0:T(8,128)S(1)}, f32[128,128]{1,0:T(8,128)S(1)}, u32[]{:S(2)}, u32[]{:S(2)}) %collective-permute-start.5) | collective-permute-done | bytes 65568 | tf_op jit(solution)/shard_map/ppermute | solution.py:29
  28.8 0.1 collective-permute-start.8
  28.9 1.3 %collective-permute-start.15 = (f32[3,128,128]{2,1,0:T(8,128)S(1)}, f32[3,128,128]{2,1,0:T(8,128)S(1)}, u32[]{:S(2)}, u32[]{:S(2)}) collective-permute-start(f32[3,128,128]{2,1,0:T(8,128)S(1)} %broadcast_select_fusion), channel_id=1, source_target_pairs={{0,2},{1,9},{4,6},{17,25},{8,10},{3,11},{12,14},{19,27},{16,18},{5... | collective-permute-start | bytes 589832 | tf_op jit(solution)/shard_map/ppermute | solution.py:29
  30.3 5.8 %collective-permute-start.9 = (f32[128,128]{1,0:T(8,128)S(1)}, f32[128,128]{1,0:T(8,128)S(1)}, u32[]{:S(2)}, u32[]{:S(2)}) collective-permute-start(f32[128,128]{1,0:T(8,128)S(1)} %broadcast_select_fusion.4), channel_id=1, source_target_pairs={{0,32},{1,33},{2,34},{3,35},{4,36},{5,37},{6,38},{7,39},{8,40},{9,... | collective-permute-start | bytes 196616 | tf_op jit(solution)/shard_map/ppermute | solution.py:29
  36.1 1.7 %collective-permute-done.15 = f32[3,128,128]{2,1,0:T(8,128)S(1)} collective-permute-done((f32[3,128,128]{2,1,0:T(8,128)S(1)}, f32[3,128,128]{2,1,0:T(8,128)S(1)}, u32[]{:S(2)}, u32[]{:S(2)}) %collective-permute-start.15) | collective-permute-done | bytes 196640 | tf_op jit(solution)/shard_map/ppermute | solution.py:29
  37.8 1.1 %collective-permute-start.18 = (f32[3,128,128]{2,1,0:T(8,128)S(1)}, f32[3,128,128]{2,1,0:T(8,128)S(1)}, u32[]{:S(2)}, u32[]{:S(2)}) collective-permute-start(f32[3,128,128]{2,1,0:T(8,128)S(1)} %broadcast_select_fusion.1), channel_id=1, source_target_pairs={{0,24},{1,7},{2,26},{9,15},{4,28},{17,23},{6,30},{25,31},{8,0},{3,... | collective-permute-start | bytes 589832 | tf_op jit(solution)/shard_map/ppermute | solution.py:29
  38.9 0.6 collective-permute-start.17
  39.5 1.3 %collective-permute-start.16 = (f32[3,128,128]{2,1,0:T(8,128)S(1)}, f32[3,128,128]{2,1,0:T(8,128)S(1)}, u32[]{:S(2)}, u32[]{:S(2)}) collective-permute-start(f32[3,128,128]{2,1,0:T(8,128)S(1)} %broadcast_select_fusion.1), channel_id=1, source_target_pairs={{0,8},{1,3},{2,10},{9,11},{4,12},{17,19},{6,14},{25,27},{8,16},{3,... | collective-permute-start | bytes 589832 | tf_op jit(solution)/shard_map/ppermute | solution.py:29
  40.8 5.3 %first_block.1 = (f32[128,128]{1,0:T(8,128)S(1)}, f32[128,128]{1,0:T(8,128)S(1)}, f32[128,128]{1,0:T(8,128)S(1)}) custom-call(s32[2]{0:T(128)S(1)} %pad_add_fusion.place, f32[128,128]{1,0:T(8,128)S(1)} %broadcast_select_fusion.10.own, f32[128,128]{1,0:T(8,128)S(1)} %collective-permute-done.9.by_row, f32[128,128]{1,0:T(8,128)S(1)} %collective-permute-done.8.by_core), custom_call_target="tpu_custom_call" | custom-call | tf_op jit(solution)/shard_map/first_block/pallas_call | solution.py:248
  46.1 2.0 %collective-permute-done.16 = f32[3,128,128]{2,1,0:T(8,128)S(1)} collective-permute-done((f32[3,128,128]{2,1,0:T(8,128)S(1)}, f32[3,128,128]{2,1,0:T(8,128)S(1)}, u32[]{:S(2)}, u32[]{:S(2)}) %collective-permute-start.16) | collective-permute-done | bytes 196640 | tf_op jit(solution)/shard_map/ppermute | solution.py:29
  48.2 0.1 collective-permute-start.19
  48.3 5.7 %collective-permute-start.10 = (f32[3,128,128]{2,1,0:T(8,128)S(1)}, f32[3,128,128]{2,1,0:T(8,128)S(1)}, u32[]{:S(2)}, u32[]{:S(2)}) collective-permute-start(f32[3,128,128]{2,1,0:T(8,128)S(1)} %broadcast_select_fusion.3.part), channel_id=1, source_target_pairs={{0,32},{1,33},{2,34},{3,35},{4,36},{5,37},{6,38},{7,39},{8,40},{9,... | collective-permute-start | bytes 589832 | tf_op jit(solution)/shard_map/ppermute | solution.py:29
  54.0 4.2 %second_block.1 = (bf16[256,256]{1,0:T(8,128)(2,1)S(1)}, bf16[256,256]{1,0:T(8,128)(2,1)S(1)}) custom-call(f32[128,128]{1,0:T(8,128)S(1)} %get-tuple-element.27.inv00, f32[128,128]{1,0:T(8,128)S(1)} %get-tuple-element.28.below, f32[128,128]{1,0:T(8,128)S(1)} %get-tuple-element.29.schur), custom_call_target="tpu_custom_call" | custom-call | tf_op jit(solution)/shard_map/second_block/pallas_call | solution.py:260
  58.3 1.1 %collective-permute-done.10.other_part = f32[3,128,128]{2,1,0:T(8,128)S(1)} collective-permute-done((f32[3,128,128]{2,1,0:T(8,128)S(1)}, f32[3,128,128]{2,1,0:T(8,128)S(1)}, u32[]{:S(2)}, u32[]{:S(2)}) %collective-permute-start.10) | collective-permute-done | bytes 196640 | tf_op jit(solution)/shard_map/ppermute | solution.py:29
  59.3 4.4 %update.1 = f32[12,3,128,128]{3,2,1,0:T(8,128)} custom-call(s32[2]{0:T(128)S(1)} %pad_add_fusion.place, bf16[256,256]{1,0:T(8,128)(2,1)S(1)} %get-tuple-element.30.high, bf16[256,256]{1,0:T(8,128)(2,1)S(1)} %get-tuple-element.31.low, f32[3,128,128]{2,1,0:T(8,128)S(1)} %broadcast_select_fusion.3.part, f32[3,128,128]{2,1,0:T(8,128)S(1)} %collective-permute-done.10.other_part, ...), custom_call_target="tpu_custom_call" | custom-call | tf_op jit(solution)/shard_map/update/pallas_call | solution.py:270
  (30 shorter events, 0.3 us)
Async XLA Ops:
  0.0 10.2 %copy-start = (f32[12,128,3,128]{3,1,2,0:T(8,128)S(1)}, f32[12,128,3,128]{3,1,2,0:T(8,128)}, u32[]{:S(2)}) copy-start(f32[12,128,3,128]{3,1,2,0:T(8,128)} %param.1) | copy-start | bytes 7077892
  1.0 0.7 %collective-permute-start = (f32[128,128]{1,0:T(8,128)S(1)}, f32[128,128]{1,0:T(8,128)S(1)}, u32[]{:S(2)}, u32[]{:S(2)}) collective-permute-start(f32[128,128]{1,0:T(8,128)S(1)} %slice_bitcast_fusion.5), channel_id=1, source_target_pairs={{0,16},{1,5},{32,48},{33,37}} | collective-permute-start | bytes 196616 | tf_op jit(solution)/shard_map/ppermute | solution.py:29
  1.7 3.9 %collective-permute-start.1 = (f32[128,128]{1,0:T(8,128)S(1)}, f32[128,128]{1,0:T(8,128)S(1)}, u32[]{:S(2)}, u32[]{:S(2)}) collective-permute-start(f32[128,128]{1,0:T(8,128)S(1)} %broadcast_select_fusion.5), channel_id=1, source_target_pairs={{0,8},{1,3},{16,24},{5,7},{32,40},{33,35},{48,56},{37,39}} | collective-permute-start | bytes 196616 | tf_op jit(solution)/shard_map/ppermute | solution.py:29
  3.6 5.8 %collective-permute-start.13 = (f32[3,128,128]{2,1,0:T(8,128)S(1)}, f32[3,128,128]{2,1,0:T(8,128)S(1)}, u32[]{:S(2)}, u32[]{:S(2)}) collective-permute-start(f32[3,128,128]{2,1,0:T(8,128)S(1)} %get-tuple-element.43), channel_id=1, source_target_pairs={{0,24},{1,7},{32,56},{33,39},{64,88},{65,71},{96,120},{97,103},{12... | collective-permute-start | bytes 589832 | tf_op jit(solution)/shard_map/ppermute | solution.py:29
  4.3 5.2 %collective-permute-start.11 = (f32[3,128,128]{2,1,0:T(8,128)S(1)}, f32[3,128,128]{2,1,0:T(8,128)}, u32[]{:S(2)}, u32[]{:S(2)}) collective-permute-start(f32[3,128,128]{2,1,0:T(8,128)S(1)} %get-tuple-element.44), channel_id=1, source_target_pairs={{0,8},{1,3},{32,40},{33,35},{64,72},{65,67},{96,104},{97,99},{128,... | collective-permute-start | bytes 589832 | tf_op jit(solution)/shard_map/ppermute | solution.py:29
  5.6 1.7 %collective-permute-start.2 = (f32[128,128]{1,0:T(8,128)S(1)}, f32[128,128]{1,0:T(8,128)S(1)}, u32[]{:S(2)}, u32[]{:S(2)}) collective-permute-start(f32[128,128]{1,0:T(8,128)S(1)} %broadcast_select_fusion.6), channel_id=1, source_target_pairs={{0,4},{1,17},{8,12},{3,19},{16,20},{5,21},{24,28},{7,23},{32,36},{... | collective-permute-start | bytes 196616 | tf_op jit(solution)/shard_map/ppermute | solution.py:29
  7.3 2.1 %collective-permute-start.3 = (f32[128,128]{1,0:T(8,128)S(1)}, f32[128,128]{1,0:T(8,128)S(1)}, u32[]{:S(2)}, u32[]{:S(2)}) collective-permute-start(f32[128,128]{1,0:T(8,128)S(1)} %broadcast_select_fusion.7), channel_id=1, source_target_pairs={{0,2},{1,9},{4,6},{17,25},{8,10},{3,11},{12,14},{19,27},{16,18},{5... | collective-permute-start | bytes 196616 | tf_op jit(solution)/shard_map/ppermute | solution.py:29
  8.1 4.2 %collective-permute-start.6 = (f32[3,128,128]{2,1,0:T(8,128)S(1)}, f32[3,128,128]{2,1,0:T(8,128)S(1)}, u32[]{:S(2)}, u32[]{:S(2)}) collective-permute-start(f32[3,128,128]{2,1,0:T(8,128)S(1)} %slice_bitcast_fusion.4), channel_id=1, source_target_pairs={{0,128},{1,129},{2,130},{3,131},{4,132},{5,133},{6,134},{7,135},{8... | collective-permute-start | bytes 589832 | tf_op jit(solution)/shard_map/ppermute | solution.py:29
  8.7 1.4 %collective-permute-start.12 = (f32[3,128,128]{2,1,0:T(8,128)S(1)}, f32[3,128,128]{2,1,0:T(8,128)S(1)}, u32[]{:S(2)}, u32[]{:S(2)}) collective-permute-start(f32[3,128,128]{2,1,0:T(8,128)S(1)} %get-tuple-element.34), channel_id=1, source_target_pairs={{0,16},{1,5},{32,48},{33,37},{64,80},{65,69},{96,112},{97,101},{12... | collective-permute-start | bytes 589832 | tf_op jit(solution)/shard_map/ppermute | solution.py:29
  9.5 1.4 %collective-permute-start.4 = (f32[128,128]{1,0:T(8,128)S(1)}, f32[128,128]{1,0:T(8,128)S(1)}, u32[]{:S(2)}, u32[]{:S(2)}) collective-permute-start(f32[128,128]{1,0:T(8,128)S(1)} %broadcast_select_fusion.8), channel_id=1, source_target_pairs={{0,128},{1,129},{2,130},{3,131},{4,132},{5,133},{6,134},{7,135},{8... | collective-permute-start | bytes 196616 | tf_op jit(solution)/shard_map/ppermute | solution.py:29
  10.2 18.7 %collective-permute-start.14 = (f32[3,128,128]{2,1,0:T(8,128)S(1)}, f32[3,128,128]{2,1,0:T(8,128)S(1)}, u32[]{:S(2)}, u32[]{:S(2)}) collective-permute-start(f32[3,128,128]{2,1,0:T(8,128)S(1)} %fusion), channel_id=1, source_target_pairs={{0,4},{1,17},{8,12},{3,19},{16,20},{5,21},{24,28},{7,23},{32,36},{... | collective-permute-start | bytes 589832 | tf_op jit(solution)/shard_map/ppermute | solution.py:29
  10.9 17.8 %collective-permute-start.5 = (f32[128,128]{1,0:T(8,128)S(1)}, f32[128,128]{1,0:T(8,128)S(1)}, u32[]{:S(2)}, u32[]{:S(2)}) collective-permute-start(f32[128,128]{1,0:T(8,128)S(1)} %broadcast_select_fusion.9), channel_id=1, source_target_pairs={{0,64},{1,65},{2,66},{3,67},{4,68},{5,69},{6,70},{7,71},{8,72},{9,... | collective-permute-start | bytes 196616 | tf_op jit(solution)/shard_map/ppermute | solution.py:29
  12.3 28.5 %collective-permute-start.7 = (f32[3,128,128]{2,1,0:T(8,128)S(1)}, f32[3,128,128]{2,1,0:T(8,128)S(1)}, u32[]{:S(2)}, u32[]{:S(2)}) collective-permute-start(f32[3,128,128]{2,1,0:T(8,128)S(1)} %broadcast_select_fusion.2), channel_id=1, source_target_pairs={{0,64},{1,65},{2,66},{3,67},{4,68},{5,69},{6,70},{7,71},{8,72},{9,... | collective-permute-start | bytes 589832 | tf_op jit(solution)/shard_map/ppermute | solution.py:29
  28.8 1.4 %collective-permute-start.8 = (f32[128,128]{1,0:T(8,128)S(1)}, f32[128,128]{1,0:T(8,128)S(1)}, u32[]{:S(2)}, u32[]{:S(2)}) collective-permute-start(f32[128,128]{1,0:T(8,128)S(1)} %broadcast_select_fusion.10.own), channel_id=1, source_target_pairs={{0,1},{1,0},{2,3},{3,2},{4,5},{5,4},{6,7},{7,6},{8,9},{9,8},{10,11... | collective-permute-start | bytes 196616 | tf_op jit(solution)/shard_map/ppermute | solution.py:29
  28.9 8.8 %collective-permute-start.15 = (f32[3,128,128]{2,1,0:T(8,128)S(1)}, f32[3,128,128]{2,1,0:T(8,128)S(1)}, u32[]{:S(2)}, u32[]{:S(2)}) collective-permute-start(f32[3,128,128]{2,1,0:T(8,128)S(1)} %broadcast_select_fusion), channel_id=1, source_target_pairs={{0,2},{1,9},{4,6},{17,25},{8,10},{3,11},{12,14},{19,27},{16,18},{5... | collective-permute-start | bytes 589832 | tf_op jit(solution)/shard_map/ppermute | solution.py:29
  30.3 10.6 %collective-permute-start.9 = (f32[128,128]{1,0:T(8,128)S(1)}, f32[128,128]{1,0:T(8,128)S(1)}, u32[]{:S(2)}, u32[]{:S(2)}) collective-permute-start(f32[128,128]{1,0:T(8,128)S(1)} %broadcast_select_fusion.4), channel_id=1, source_target_pairs={{0,32},{1,33},{2,34},{3,35},{4,36},{5,37},{6,38},{7,39},{8,40},{9,... | collective-permute-start | bytes 196616 | tf_op jit(solution)/shard_map/ppermute | solution.py:29
  37.8 8.3 %collective-permute-start.18 = (f32[3,128,128]{2,1,0:T(8,128)S(1)}, f32[3,128,128]{2,1,0:T(8,128)S(1)}, u32[]{:S(2)}, u32[]{:S(2)}) collective-permute-start(f32[3,128,128]{2,1,0:T(8,128)S(1)} %broadcast_select_fusion.1), channel_id=1, source_target_pairs={{0,24},{1,7},{2,26},{9,15},{4,28},{17,23},{6,30},{25,31},{8,0},{3,... | collective-permute-start | bytes 589832 | tf_op jit(solution)/shard_map/ppermute | solution.py:29
  38.9 7.3 %collective-permute-start.17 = (f32[3,128,128]{2,1,0:T(8,128)S(1)}, f32[3,128,128]{2,1,0:T(8,128)S(1)}, u32[]{:S(2)}, u32[]{:S(2)}) collective-permute-start(f32[3,128,128]{2,1,0:T(8,128)S(1)} %broadcast_select_fusion.1), channel_id=1, source_target_pairs={{0,16},{1,5},{2,18},{9,13},{4,20},{17,21},{6,22},{25,29},{8,24},{3... | collective-permute-start | bytes 589832 | tf_op jit(solution)/shard_map/ppermute | solution.py:29
  39.5 8.7 %collective-permute-start.16 = (f32[3,128,128]{2,1,0:T(8,128)S(1)}, f32[3,128,128]{2,1,0:T(8,128)S(1)}, u32[]{:S(2)}, u32[]{:S(2)}) collective-permute-start(f32[3,128,128]{2,1,0:T(8,128)S(1)} %broadcast_select_fusion.1), channel_id=1, source_target_pairs={{0,8},{1,3},{2,10},{9,11},{4,12},{17,19},{6,14},{25,27},{8,16},{3,... | collective-permute-start | bytes 589832 | tf_op jit(solution)/shard_map/ppermute | solution.py:29
  48.2 11.1 %collective-permute-start.19 = (f32[4,3,128,128]{3,2,1,0:T(8,128)S(1)}, f32[4,3,128,128]{3,2,1,0:T(8,128)S(1)}, u32[]{:S(2)}, u32[]{:S(2)}) collective-permute-start(f32[4,3,128,128]{3,2,1,0:T(8,128)S(1)} %pad_maximum_fusion.near), channel_id=1, source_target_pairs={{0,1},{1,0},{2,3},{3,2},{4,5},{5,4},{6,7},{7,6},{8,9},{9,8},{10,11... | collective-permute-start | bytes 2359304 | tf_op jit(solution)/shard_map/ppermute | solution.py:29
  48.3 11.0 %collective-permute-start.10 = (f32[3,128,128]{2,1,0:T(8,128)S(1)}, f32[3,128,128]{2,1,0:T(8,128)S(1)}, u32[]{:S(2)}, u32[]{:S(2)}) collective-permute-start(f32[3,128,128]{2,1,0:T(8,128)S(1)} %broadcast_select_fusion.3.part), channel_id=1, source_target_pairs={{0,32},{1,33},{2,34},{3,35},{4,36},{5,37},{6,38},{7,39},{8,40},{9,... | collective-permute-start | bytes 589832 | tf_op jit(solution)/shard_map/ppermute | solution.py:29

commit v5 on v4

--- a/solution.py
+++ b/solution.py
@@ -105,9 +105,9 @@
 
 
 def second_block(inv00, below, schur, high, low):
-    mixed = exact(below[...], inv00[...])
+    mixed = halves(product(halves(below[...]), halves(inv00[...]), False))
     inv11 = inverse_factor(schur[...])
-    inv10 = -exact(inv11, mixed)
+    inv10 = -product(halves(inv11), mixed, False)
     zero = jnp.zeros((TB, TB), jnp.float32)
     for i, line in enumerate(((inv00[...], zero), (inv10, inv11))):
         for j, value in enumerate(line):

time: 65.2 us -> 65.2 us (level)
  no operation moved by 1% of the time
where the time goes in v5:
time: 65.2 us; the launch traced here: 63.9 us
  starting transfers between devices  26 us (40%)
  waiting for transfers between devices  20.1 us (31%)
  Pallas kernels  13.8 us (21%)
  local copies, waits for them, and re-layouts  3.1 us (5%)
    ppermute x20, starting transfers between devices, send(): return lax.ppermute(value, ('row', 'col'), pairs)  26 us
    ppermute x20, waiting for transfers between devices, send(): return lax.ppermute(value, ('row', 'col'), pairs)  20.1 us
    pallas_call x1, Pallas kernels, shards(): pl.pallas_call(first_block, out_shape=[tile] * 3, in_specs=[smem] + [vmem...  5.29 us
    pallas_call x1, Pallas kernels, shards(): pl.pallas_call(update, out_shape=jax.ShapeDtypeStruct(tiles.shape, tiles....  4.42 us
    pallas_call x1, Pallas kernels, shards(): pl.pallas_call(second_block, out_shape=[inverse] * 2, in_specs=[vmem] * 3...  4.07 us
  transfers between devices with their start and end apart: 20, of which 4 were waited for; matrix products, arithmetic and copies ran while one was open for 4% of the time, Pallas kernels for 15%

profile of v5, /device:TPU:200, one launch (start us, length us, event | category | flops | bytes accessed | tf_op | source)
XLA Modules:
  0.0 63.9 jit_solution(11423096529536259229)
XLA Ops:
  0.0 1.0 %slice_bitcast_fusion.5 = f32[128,128]{1,0:T(8,128)S(1)} fusion(f32[12,3,128,128]{3,2,1,0:T(8,128)} %bitcast.28), kind=kLoop, calls=%fused_computation.11 | loop fusion | bytes 131072 | tf_op jit(solution)/shard_map/squeeze | solution.py:201
  1.0 0.7 %collective-permute-start = (f32[128,128]{1,0:T(8,128)S(1)}, f32[128,128]{1,0:T(8,128)S(1)}, u32[]{:S(2)}, u32[]{:S(2)}) collective-permute-start(f32[128,128]{1,0:T(8,128)S(1)} %slice_bitcast_fusion.5), channel_id=1, source_target_pairs={{0,16},{1,5},{32,48},{33,37}} | collective-permute-start | bytes 196616 | tf_op jit(solution)/shard_map/ppermute | solution.py:29
  1.7 0.7 %collective-permute-start.1 = (f32[128,128]{1,0:T(8,128)S(1)}, f32[128,128]{1,0:T(8,128)S(1)}, u32[]{:S(2)}, u32[]{:S(2)}) collective-permute-start(f32[128,128]{1,0:T(8,128)S(1)} %broadcast_select_fusion.5), channel_id=1, source_target_pairs={{0,8},{1,3},{16,24},{5,7},{32,40},{33,35},{48,56},{37,39}} | collective-permute-start | bytes 196616 | tf_op jit(solution)/shard_map/ppermute | solution.py:29
  2.4 1.2 %slice_bitcast_fusion = (f32[3,128,128]{2,1,0:T(8,128)S(1)}, f32[3,128,128]{2,1,0:T(8,128)S(1)}, f32[3,128,128]{2,1,0:T(8,128)S(1)}) fusion(f32[12,3,128,128]{3,2,1,0:T(8,128)} %bitcast.29), kind=kLoop, calls=%fused_computation.1 | loop fusion | bytes 1179648 | tf_op jit(solution)/shard_map/squeeze | solution.py:204
  3.6 0.7 %collective-permute-start.13 = (f32[3,128,128]{2,1,0:T(8,128)S(1)}, f32[3,128,128]{2,1,0:T(8,128)S(1)}, u32[]{:S(2)}, u32[]{:S(2)}) collective-permute-start(f32[3,128,128]{2,1,0:T(8,128)S(1)} %get-tuple-element.43), channel_id=1, source_target_pairs={{0,24},{1,7},{32,56},{33,39},{64,88},{65,71},{96,120},{97,103},{12... | collective-permute-start | bytes 589832 | tf_op jit(solution)/shard_map/ppermute | solution.py:29
  4.3 1.3 %collective-permute-start.11 = (f32[3,128,128]{2,1,0:T(8,128)S(1)}, f32[3,128,128]{2,1,0:T(8,128)}, u32[]{:S(2)}, u32[]{:S(2)}) collective-permute-start(f32[3,128,128]{2,1,0:T(8,128)S(1)} %get-tuple-element.44), channel_id=1, source_target_pairs={{0,8},{1,3},{32,40},{33,35},{64,72},{65,67},{96,104},{97,99},{128,... | collective-permute-start | bytes 589832 | tf_op jit(solution)/shard_map/ppermute | solution.py:29
  5.6 0.7 %collective-permute-start.2 = (f32[128,128]{1,0:T(8,128)S(1)}, f32[128,128]{1,0:T(8,128)S(1)}, u32[]{:S(2)}, u32[]{:S(2)}) collective-permute-start(f32[128,128]{1,0:T(8,128)S(1)} %broadcast_select_fusion.6), channel_id=1, source_target_pairs={{0,4},{1,17},{8,12},{3,19},{16,20},{5,21},{24,28},{7,23},{32,36},{... | collective-permute-start | bytes 196616 | tf_op jit(solution)/shard_map/ppermute | solution.py:29
  6.3 0.9 %slice_bitcast_fusion.4 = f32[3,128,128]{2,1,0:T(8,128)S(1)} fusion(f32[12,3,128,128]{3,2,1,0:T(8,128)} %bitcast.30), kind=kLoop, calls=%fused_computation.6 | loop fusion | bytes 393216 | tf_op jit(solution)/shard_map/squeeze | solution.py:200
  7.3 0.7 %collective-permute-start.3 = (f32[128,128]{1,0:T(8,128)S(1)}, f32[128,128]{1,0:T(8,128)S(1)}, u32[]{:S(2)}, u32[]{:S(2)}) collective-permute-start(f32[128,128]{1,0:T(8,128)S(1)} %broadcast_select_fusion.7), channel_id=1, source_target_pairs={{0,2},{1,9},{4,6},{17,25},{8,10},{3,11},{12,14},{19,27},{16,18},{5... | collective-permute-start | bytes 196616 | tf_op jit(solution)/shard_map/ppermute | solution.py:29
  8.0 0.1 pad_add_fusion.place
  8.1 0.7 %collective-permute-start.6 = (f32[3,128,128]{2,1,0:T(8,128)S(1)}, f32[3,128,128]{2,1,0:T(8,128)S(1)}, u32[]{:S(2)}, u32[]{:S(2)}) collective-permute-start(f32[3,128,128]{2,1,0:T(8,128)S(1)} %slice_bitcast_fusion.4), channel_id=1, source_target_pairs={{0,128},{1,129},{2,130},{3,131},{4,132},{5,133},{6,134},{7,135},{8... | collective-permute-start | bytes 589832 | tf_op jit(solution)/shard_map/ppermute | solution.py:29
  8.7 0.7 %collective-permute-start.12 = (f32[3,128,128]{2,1,0:T(8,128)S(1)}, f32[3,128,128]{2,1,0:T(8,128)S(1)}, u32[]{:S(2)}, u32[]{:S(2)}) collective-permute-start(f32[3,128,128]{2,1,0:T(8,128)S(1)} %get-tuple-element.34), channel_id=1, source_target_pairs={{0,16},{1,5},{32,48},{33,37},{64,80},{65,69},{96,112},{97,101},{12... | collective-permute-start | bytes 589832 | tf_op jit(solution)/shard_map/ppermute | solution.py:29
  9.5 0.7 %collective-permute-start.4 = (f32[128,128]{1,0:T(8,128)S(1)}, f32[128,128]{1,0:T(8,128)S(1)}, u32[]{:S(2)}, u32[]{:S(2)}) collective-permute-start(f32[128,128]{1,0:T(8,128)S(1)} %broadcast_select_fusion.8), channel_id=1, source_target_pairs={{0,128},{1,129},{2,130},{3,131},{4,132},{5,133},{6,134},{7,135},{8... | collective-permute-start | bytes 196616 | tf_op jit(solution)/shard_map/ppermute | solution.py:29
  10.2 0.1 fusion
  10.2 0.7 %collective-permute-start.14 = (f32[3,128,128]{2,1,0:T(8,128)S(1)}, f32[3,128,128]{2,1,0:T(8,128)S(1)}, u32[]{:S(2)}, u32[]{:S(2)}) collective-permute-start(f32[3,128,128]{2,1,0:T(8,128)S(1)} %fusion), channel_id=1, source_target_pairs={{0,4},{1,17},{8,12},{3,19},{16,20},{5,21},{24,28},{7,23},{32,36},{... | collective-permute-start | bytes 589832 | tf_op jit(solution)/shard_map/ppermute | solution.py:29
  10.9 1.3 %collective-permute-start.5 = (f32[128,128]{1,0:T(8,128)S(1)}, f32[128,128]{1,0:T(8,128)S(1)}, u32[]{:S(2)}, u32[]{:S(2)}) collective-permute-start(f32[128,128]{1,0:T(8,128)S(1)} %broadcast_select_fusion.9), channel_id=1, source_target_pairs={{0,64},{1,65},{2,66},{3,67},{4,68},{5,69},{6,70},{7,71},{8,72},{9,... | collective-permute-start | bytes 196616 | tf_op jit(solution)/shard_map/ppermute | solution.py:29
  12.3 1.3 %collective-permute-start.7 = (f32[3,128,128]{2,1,0:T(8,128)S(1)}, f32[3,128,128]{2,1,0:T(8,128)S(1)}, u32[]{:S(2)}, u32[]{:S(2)}) collective-permute-start(f32[3,128,128]{2,1,0:T(8,128)S(1)} %broadcast_select_fusion.2), channel_id=1, source_target_pairs={{0,64},{1,65},{2,66},{3,67},{4,68},{5,69},{6,70},{7,71},{8,72},{9,... | collective-permute-start | bytes 589832 | tf_op jit(solution)/shard_map/ppermute | solution.py:29
  13.6 15.2 %collective-permute-done.5 = f32[128,128]{1,0:T(8,128)S(1)} collective-permute-done((f32[128,128]{1,0:T(8,128)S(1)}, f32[128,128]{1,0:T(8,128)S(1)}, u32[]{:S(2)}, u32[]{:S(2)}) %collective-permute-start.5) | collective-permute-done | bytes 65568 | tf_op jit(solution)/shard_map/ppermute | solution.py:29
  28.8 0.1 collective-permute-start.8
  28.9 1.3 %collective-permute-start.15 = (f32[3,128,128]{2,1,0:T(8,128)S(1)}, f32[3,128,128]{2,1,0:T(8,128)S(1)}, u32[]{:S(2)}, u32[]{:S(2)}) collective-permute-start(f32[3,128,128]{2,1,0:T(8,128)S(1)} %broadcast_select_fusion), channel_id=1, source_target_pairs={{0,2},{1,9},{4,6},{17,25},{8,10},{3,11},{12,14},{19,27},{16,18},{5... | collective-permute-start | bytes 589832 | tf_op jit(solution)/shard_map/ppermute | solution.py:29
  30.3 5.8 %collective-permute-start.9 = (f32[128,128]{1,0:T(8,128)S(1)}, f32[128,128]{1,0:T(8,128)S(1)}, u32[]{:S(2)}, u32[]{:S(2)}) collective-permute-start(f32[128,128]{1,0:T(8,128)S(1)} %broadcast_select_fusion.4), channel_id=1, source_target_pairs={{0,32},{1,33},{2,34},{3,35},{4,36},{5,37},{6,38},{7,39},{8,40},{9,... | collective-permute-start | bytes 196616 | tf_op jit(solution)/shard_map/ppermute | solution.py:29
  36.1 1.7 %collective-permute-done.15 = f32[3,128,128]{2,1,0:T(8,128)S(1)} collective-permute-done((f32[3,128,128]{2,1,0:T(8,128)S(1)}, f32[3,128,128]{2,1,0:T(8,128)S(1)}, u32[]{:S(2)}, u32[]{:S(2)}) %collective-permute-start.15) | collective-permute-done | bytes 196640 | tf_op jit(solution)/shard_map/ppermute | solution.py:29
  37.8 1.1 %collective-permute-start.18 = (f32[3,128,128]{2,1,0:T(8,128)S(1)}, f32[3,128,128]{2,1,0:T(8,128)S(1)}, u32[]{:S(2)}, u32[]{:S(2)}) collective-permute-start(f32[3,128,128]{2,1,0:T(8,128)S(1)} %broadcast_select_fusion.1), channel_id=1, source_target_pairs={{0,24},{1,7},{2,26},{9,15},{4,28},{17,23},{6,30},{25,31},{8,0},{3,... | collective-permute-start | bytes 589832 | tf_op jit(solution)/shard_map/ppermute | solution.py:29
  38.9 0.6 collective-permute-start.17
  39.5 1.3 %collective-permute-start.16 = (f32[3,128,128]{2,1,0:T(8,128)S(1)}, f32[3,128,128]{2,1,0:T(8,128)S(1)}, u32[]{:S(2)}, u32[]{:S(2)}) collective-permute-start(f32[3,128,128]{2,1,0:T(8,128)S(1)} %broadcast_select_fusion.1), channel_id=1, source_target_pairs={{0,8},{1,3},{2,10},{9,11},{4,12},{17,19},{6,14},{25,27},{8,16},{3,... | collective-permute-start | bytes 589832 | tf_op jit(solution)/shard_map/ppermute | solution.py:29
  40.8 5.3 %first_block.1 = (f32[128,128]{1,0:T(8,128)S(1)}, f32[128,128]{1,0:T(8,128)S(1)}, f32[128,128]{1,0:T(8,128)S(1)}) custom-call(s32[2]{0:T(128)S(1)} %pad_add_fusion.place, f32[128,128]{1,0:T(8,128)S(1)} %broadcast_select_fusion.10.own, f32[128,128]{1,0:T(8,128)S(1)} %collective-permute-done.9.by_row, f32[128,128]{1,0:T(8,128)S(1)} %collective-permute-done.8.by_core), custom_call_target="tpu_custom_call" | custom-call | tf_op jit(solution)/shard_map/first_block/pallas_call | solution.py:248
  46.1 2.0 %collective-permute-done.16 = f32[3,128,128]{2,1,0:T(8,128)S(1)} collective-permute-done((f32[3,128,128]{2,1,0:T(8,128)S(1)}, f32[3,128,128]{2,1,0:T(8,128)S(1)}, u32[]{:S(2)}, u32[]{:S(2)}) %collective-permute-start.16) | collective-permute-done | bytes 196640 | tf_op jit(solution)/shard_map/ppermute | solution.py:29
  48.2 0.1 collective-permute-start.19
  48.3 5.7 %collective-permute-start.10 = (f32[3,128,128]{2,1,0:T(8,128)S(1)}, f32[3,128,128]{2,1,0:T(8,128)S(1)}, u32[]{:S(2)}, u32[]{:S(2)}) collective-permute-start(f32[3,128,128]{2,1,0:T(8,128)S(1)} %broadcast_select_fusion.3.part), channel_id=1, source_target_pairs={{0,32},{1,33},{2,34},{3,35},{4,36},{5,37},{6,38},{7,39},{8,40},{9,... | collective-permute-start | bytes 589832 | tf_op jit(solution)/shard_map/ppermute | solution.py:29
  54.0 4.1 %second_block.1 = (bf16[256,256]{1,0:T(8,128)(2,1)S(1)}, bf16[256,256]{1,0:T(8,128)(2,1)S(1)}) custom-call(f32[128,128]{1,0:T(8,128)S(1)} %get-tuple-element.27.inv00, f32[128,128]{1,0:T(8,128)S(1)} %get-tuple-element.28.below, f32[128,128]{1,0:T(8,128)S(1)} %get-tuple-element.29.schur), custom_call_target="tpu_custom_call" | custom-call | tf_op jit(solution)/shard_map/second_block/pallas_call | solution.py:260
  58.1 1.2 %collective-permute-done.10.other_part = f32[3,128,128]{2,1,0:T(8,128)S(1)} collective-permute-done((f32[3,128,128]{2,1,0:T(8,128)S(1)}, f32[3,128,128]{2,1,0:T(8,128)S(1)}, u32[]{:S(2)}, u32[]{:S(2)}) %collective-permute-start.10) | collective-permute-done | bytes 196640 | tf_op jit(solution)/shard_map/ppermute | solution.py:29
  59.3 4.4 %update.1 = f32[12,3,128,128]{3,2,1,0:T(8,128)} custom-call(s32[2]{0:T(128)S(1)} %pad_add_fusion.place, bf16[256,256]{1,0:T(8,128)(2,1)S(1)} %get-tuple-element.30.high, bf16[256,256]{1,0:T(8,128)(2,1)S(1)} %get-tuple-element.31.low, f32[3,128,128]{2,1,0:T(8,128)S(1)} %broadcast_select_fusion.3.part, f32[3,128,128]{2,1,0:T(8,128)S(1)} %collective-permute-done.10.other_part, ...), custom_call_target="tpu_custom_call" | custom-call | tf_op jit(solution)/shard_map/update/pallas_call | solution.py:270
  (30 shorter events, 0.3 us)
Async XLA Ops:
  0.0 10.2 %copy-start = (f32[12,128,3,128]{3,1,2,0:T(8,128)S(1)}, f32[12,128,3,128]{3,1,2,0:T(8,128)}, u32[]{:S(2)}) copy-start(f32[12,128,3,128]{3,1,2,0:T(8,128)} %param.1) | copy-start | bytes 7077892
  1.0 0.7 %collective-permute-start = (f32[128,128]{1,0:T(8,128)S(1)}, f32[128,128]{1,0:T(8,128)S(1)}, u32[]{:S(2)}, u32[]{:S(2)}) collective-permute-start(f32[128,128]{1,0:T(8,128)S(1)} %slice_bitcast_fusion.5), channel_id=1, source_target_pairs={{0,16},{1,5},{32,48},{33,37}} | collective-permute-start | bytes 196616 | tf_op jit(solution)/shard_map/ppermute | solution.py:29
  1.7 3.9 %collective-permute-start.1 = (f32[128,128]{1,0:T(8,128)S(1)}, f32[128,128]{1,0:T(8,128)S(1)}, u32[]{:S(2)}, u32[]{:S(2)}) collective-permute-start(f32[128,128]{1,0:T(8,128)S(1)} %broadcast_select_fusion.5), channel_id=1, source_target_pairs={{0,8},{1,3},{16,24},{5,7},{32,40},{33,35},{48,56},{37,39}} | collective-permute-start | bytes 196616 | tf_op jit(solution)/shard_map/ppermute | solution.py:29
  3.6 5.8 %collective-permute-start.13 = (f32[3,128,128]{2,1,0:T(8,128)S(1)}, f32[3,128,128]{2,1,0:T(8,128)S(1)}, u32[]{:S(2)}, u32[]{:S(2)}) collective-permute-start(f32[3,128,128]{2,1,0:T(8,128)S(1)} %get-tuple-element.43), channel_id=1, source_target_pairs={{0,24},{1,7},{32,56},{33,39},{64,88},{65,71},{96,120},{97,103},{12... | collective-permute-start | bytes 589832 | tf_op jit(solution)/shard_map/ppermute | solution.py:29
  4.3 5.2 %collective-permute-start.11 = (f32[3,128,128]{2,1,0:T(8,128)S(1)}, f32[3,128,128]{2,1,0:T(8,128)}, u32[]{:S(2)}, u32[]{:S(2)}) collective-permute-start(f32[3,128,128]{2,1,0:T(8,128)S(1)} %get-tuple-element.44), channel_id=1, source_target_pairs={{0,8},{1,3},{32,40},{33,35},{64,72},{65,67},{96,104},{97,99},{128,... | collective-permute-start | bytes 589832 | tf_op jit(solution)/shard_map/ppermute | solution.py:29
  5.6 1.7 %collective-permute-start.2 = (f32[128,128]{1,0:T(8,128)S(1)}, f32[128,128]{1,0:T(8,128)S(1)}, u32[]{:S(2)}, u32[]{:S(2)}) collective-permute-start(f32[128,128]{1,0:T(8,128)S(1)} %broadcast_select_fusion.6), channel_id=1, source_target_pairs={{0,4},{1,17},{8,12},{3,19},{16,20},{5,21},{24,28},{7,23},{32,36},{... | collective-permute-start | bytes 196616 | tf_op jit(solution)/shard_map/ppermute | solution.py:29
  7.3 2.1 %collective-permute-start.3 = (f32[128,128]{1,0:T(8,128)S(1)}, f32[128,128]{1,0:T(8,128)S(1)}, u32[]{:S(2)}, u32[]{:S(2)}) collective-permute-start(f32[128,128]{1,0:T(8,128)S(1)} %broadcast_select_fusion.7), channel_id=1, source_target_pairs={{0,2},{1,9},{4,6},{17,25},{8,10},{3,11},{12,14},{19,27},{16,18},{5... | collective-permute-start | bytes 196616 | tf_op jit(solution)/shard_map/ppermute | solution.py:29
  8.1 4.2 %collective-permute-start.6 = (f32[3,128,128]{2,1,0:T(8,128)S(1)}, f32[3,128,128]{2,1,0:T(8,128)S(1)}, u32[]{:S(2)}, u32[]{:S(2)}) collective-permute-start(f32[3,128,128]{2,1,0:T(8,128)S(1)} %slice_bitcast_fusion.4), channel_id=1, source_target_pairs={{0,128},{1,129},{2,130},{3,131},{4,132},{5,133},{6,134},{7,135},{8... | collective-permute-start | bytes 589832 | tf_op jit(solution)/shard_map/ppermute | solution.py:29
  8.7 1.4 %collective-permute-start.12 = (f32[3,128,128]{2,1,0:T(8,128)S(1)}, f32[3,128,128]{2,1,0:T(8,128)S(1)}, u32[]{:S(2)}, u32[]{:S(2)}) collective-permute-start(f32[3,128,128]{2,1,0:T(8,128)S(1)} %get-tuple-element.34), channel_id=1, source_target_pairs={{0,16},{1,5},{32,48},{33,37},{64,80},{65,69},{96,112},{97,101},{12... | collective-permute-start | bytes 589832 | tf_op jit(solution)/shard_map/ppermute | solution.py:29
  9.5 1.4 %collective-permute-start.4 = (f32[128,128]{1,0:T(8,128)S(1)}, f32[128,128]{1,0:T(8,128)S(1)}, u32[]{:S(2)}, u32[]{:S(2)}) collective-permute-start(f32[128,128]{1,0:T(8,128)S(1)} %broadcast_select_fusion.8), channel_id=1, source_target_pairs={{0,128},{1,129},{2,130},{3,131},{4,132},{5,133},{6,134},{7,135},{8... | collective-permute-start | bytes 196616 | tf_op jit(solution)/shard_map/ppermute | solution.py:29
  10.2 18.7 %collective-permute-start.14 = (f32[3,128,128]{2,1,0:T(8,128)S(1)}, f32[3,128,128]{2,1,0:T(8,128)S(1)}, u32[]{:S(2)}, u32[]{:S(2)}) collective-permute-start(f32[3,128,128]{2,1,0:T(8,128)S(1)} %fusion), channel_id=1, source_target_pairs={{0,4},{1,17},{8,12},{3,19},{16,20},{5,21},{24,28},{7,23},{32,36},{... | collective-permute-start | bytes 589832 | tf_op jit(solution)/shard_map/ppermute | solution.py:29
  10.9 17.8 %collective-permute-start.5 = (f32[128,128]{1,0:T(8,128)S(1)}, f32[128,128]{1,0:T(8,128)S(1)}, u32[]{:S(2)}, u32[]{:S(2)}) collective-permute-start(f32[128,128]{1,0:T(8,128)S(1)} %broadcast_select_fusion.9), channel_id=1, source_target_pairs={{0,64},{1,65},{2,66},{3,67},{4,68},{5,69},{6,70},{7,71},{8,72},{9,... | collective-permute-start | bytes 196616 | tf_op jit(solution)/shard_map/ppermute | solution.py:29
  12.3 28.5 %collective-permute-start.7 = (f32[3,128,128]{2,1,0:T(8,128)S(1)}, f32[3,128,128]{2,1,0:T(8,128)S(1)}, u32[]{:S(2)}, u32[]{:S(2)}) collective-permute-start(f32[3,128,128]{2,1,0:T(8,128)S(1)} %broadcast_select_fusion.2), channel_id=1, source_target_pairs={{0,64},{1,65},{2,66},{3,67},{4,68},{5,69},{6,70},{7,71},{8,72},{9,... | collective-permute-start | bytes 589832 | tf_op jit(solution)/shard_map/ppermute | solution.py:29
  28.8 1.4 %collective-permute-start.8 = (f32[128,128]{1,0:T(8,128)S(1)}, f32[128,128]{1,0:T(8,128)S(1)}, u32[]{:S(2)}, u32[]{:S(2)}) collective-permute-start(f32[128,128]{1,0:T(8,128)S(1)} %broadcast_select_fusion.10.own), channel_id=1, source_target_pairs={{0,1},{1,0},{2,3},{3,2},{4,5},{5,4},{6,7},{7,6},{8,9},{9,8},{10,11... | collective-permute-start | bytes 196616 | tf_op jit(solution)/shard_map/ppermute | solution.py:29
  28.9 8.8 %collective-permute-start.15 = (f32[3,128,128]{2,1,0:T(8,128)S(1)}, f32[3,128,128]{2,1,0:T(8,128)S(1)}, u32[]{:S(2)}, u32[]{:S(2)}) collective-permute-start(f32[3,128,128]{2,1,0:T(8,128)S(1)} %broadcast_select_fusion), channel_id=1, source_target_pairs={{0,2},{1,9},{4,6},{17,25},{8,10},{3,11},{12,14},{19,27},{16,18},{5... | collective-permute-start | bytes 589832 | tf_op jit(solution)/shard_map/ppermute | solution.py:29
  30.3 10.6 %collective-permute-start.9 = (f32[128,128]{1,0:T(8,128)S(1)}, f32[128,128]{1,0:T(8,128)S(1)}, u32[]{:S(2)}, u32[]{:S(2)}) collective-permute-start(f32[128,128]{1,0:T(8,128)S(1)} %broadcast_select_fusion.4), channel_id=1, source_target_pairs={{0,32},{1,33},{2,34},{3,35},{4,36},{5,37},{6,38},{7,39},{8,40},{9,... | collective-permute-start | bytes 196616 | tf_op jit(solution)/shard_map/ppermute | solution.py:29
  37.8 8.3 %collective-permute-start.18 = (f32[3,128,128]{2,1,0:T(8,128)S(1)}, f32[3,128,128]{2,1,0:T(8,128)S(1)}, u32[]{:S(2)}, u32[]{:S(2)}) collective-permute-start(f32[3,128,128]{2,1,0:T(8,128)S(1)} %broadcast_select_fusion.1), channel_id=1, source_target_pairs={{0,24},{1,7},{2,26},{9,15},{4,28},{17,23},{6,30},{25,31},{8,0},{3,... | collective-permute-start | bytes 589832 | tf_op jit(solution)/shard_map/ppermute | solution.py:29
  38.9 7.3 %collective-permute-start.17 = (f32[3,128,128]{2,1,0:T(8,128)S(1)}, f32[3,128,128]{2,1,0:T(8,128)S(1)}, u32[]{:S(2)}, u32[]{:S(2)}) collective-permute-start(f32[3,128,128]{2,1,0:T(8,128)S(1)} %broadcast_select_fusion.1), channel_id=1, source_target_pairs={{0,16},{1,5},{2,18},{9,13},{4,20},{17,21},{6,22},{25,29},{8,24},{3... | collective-permute-start | bytes 589832 | tf_op jit(solution)/shard_map/ppermute | solution.py:29
  39.5 8.7 %collective-permute-start.16 = (f32[3,128,128]{2,1,0:T(8,128)S(1)}, f32[3,128,128]{2,1,0:T(8,128)S(1)}, u32[]{:S(2)}, u32[]{:S(2)}) collective-permute-start(f32[3,128,128]{2,1,0:T(8,128)S(1)} %broadcast_select_fusion.1), channel_id=1, source_target_pairs={{0,8},{1,3},{2,10},{9,11},{4,12},{17,19},{6,14},{25,27},{8,16},{3,... | collective-permute-start | bytes 589832 | tf_op jit(solution)/shard_map/ppermute | solution.py:29
  48.2 11.1 %collective-permute-start.19 = (f32[4,3,128,128]{3,2,1,0:T(8,128)S(1)}, f32[4,3,128,128]{3,2,1,0:T(8,128)S(1)}, u32[]{:S(2)}, u32[]{:S(2)}) collective-permute-start(f32[4,3,128,128]{3,2,1,0:T(8,128)S(1)} %pad_maximum_fusion.near), channel_id=1, source_target_pairs={{0,1},{1,0},{2,3},{3,2},{4,5},{5,4},{6,7},{7,6},{8,9},{9,8},{10,11... | collective-permute-start | bytes 2359304 | tf_op jit(solution)/shard_map/ppermute | solution.py:29
  48.3 11.0 %collective-permute-start.10 = (f32[3,128,128]{2,1,0:T(8,128)S(1)}, f32[3,128,128]{2,1,0:T(8,128)S(1)}, u32[]{:S(2)}, u32[]{:S(2)}) collective-permute-start(f32[3,128,128]{2,1,0:T(8,128)S(1)} %broadcast_select_fusion.3.part), channel_id=1, source_target_pairs={{0,32},{1,33},{2,34},{3,35},{4,36},{5,37},{6,38},{7,39},{8,40},{9,... | collective-permute-start | bytes 589832 | tf_op jit(solution)/shard_map/ppermute | solution.py:29
